TPU v7x, 512 devices: a whole 4x8x8 slice. The times are simulated.
512 devices in a mesh: gz: 128 (over z, y, core), gy: 2 (over x_hi), gx: 2 (over x_lo).
Axes of the slice: x: 4 (x_hi: 2, x_lo: 2; x = x_hi * 2 + x_lo), y: 8, z: 8, core: 2. Of those that a mesh axis runs over, the one named last changes fastest.
Arguments:
- density: float32 [256, 512, 512], P('gz', 'gy', 'gx'), may hold values from -6 to 6
- bins: int32 [256, 512, 512], P('gz', 'gy', 'gx'), may hold values from 0 to 255
- tf_color: bfloat16 [3, 256], replicated, may hold values from 0.5 to 4
- tf_opacity: bfloat16 [1, 256], replicated, may hold values from 0.0009994507 to 0.039794922
- view_back: int32 [512], P('gx'), may hold values from 0 to 1
Outputs:
- image: float32 [4, 2, 128, 2, 512], P(None, 'gy', 'gz', None, 'gx')
All inputs are finite; a program needn't handle non-finite values.
Results may differ from a plain program's by a relative error of at most 0.0003.
Values sent between devices are 32-bit elements; how exact they have to be, the bound alone decides.
A program may use at most 64 MiB of HBM per device.

v0:
```python
import jax
import jax.numpy as jnp
from jax import lax
from jax.sharding import PartitionSpec as P

AMBIENT = 0.2
DIFFUSE = 1.6
LIGHT_X = 0.36
LIGHT_Y = 0.48
LIGHT_Z = 0.8


def padded_2(cells, sides, width):
    for axis, dim in sides:
        count = lax.axis_size(axis)
        ends = count - 1
        head = lax.slice_in_dim(cells, 0, width, axis=dim)
        tail = lax.slice_in_dim(cells, cells.shape[dim] - width, cells.shape[dim], axis=dim)
        cells = jnp.concatenate(
            [
                lax.ppermute(tail, axis, [(i, (i + 1) % count) for i in range(ends)]),
                cells,
                lax.ppermute(head, axis, [((i + 1) % count, i) for i in range(ends)]),
            ],
            axis=dim,
        )
    return cells


def partner(block, axis, distance):
    count = lax.axis_size(axis)
    route = []
    for low in range(count):
        high = low | 1 << distance
        if high != low and high < count:
            route += [(low, high), (high, low)]
    return lax.ppermute(block, axis, route)


def stack_over(front, back):
    return front + (1.0 - front[3:4]) * back


def depth_pair(lower, upper, view_flag):
    front = jnp.where(view_flag == 1, upper, lower)
    back = jnp.where(view_flag == 1, lower, upper)
    return stack_over(front, back)


def local(density, bins, tf_color, tf_opacity, view_back):
    depth, rows, cols = density.shape
    padded = padded_2(density, (("gz", 0), ("gy", 1), ("gx", 2)), 1)
    grad_z = (padded[2:, 1:-1, 1:-1] - padded[:-2, 1:-1, 1:-1]) * 0.5
    grad_y = (padded[1:-1, 2:, 1:-1] - padded[1:-1, :-2, 1:-1]) * 0.5
    grad_x = (padded[1:-1, 1:-1, 2:] - padded[1:-1, 1:-1, :-2]) * 0.5
    shade = AMBIENT + DIFFUSE * jnp.abs(
        grad_x * LIGHT_X + grad_y * LIGHT_Y + grad_z * LIGHT_Z
    ) / jnp.sqrt(1.0 + grad_x * grad_x + grad_y * grad_y + grad_z * grad_z)
    table = jnp.concatenate([tf_color, tf_opacity], axis=0)
    entries = table.shape[1]
    total = depth * rows * cols
    block = min(total, 8192)
    flat_bins = bins.reshape(total // block, block)
    entry_ids = lax.broadcasted_iota(jnp.int32, (entries, block), 0)

    def lookup(block_bins):
        onehot = (entry_ids == block_bins[None, :]).astype(jnp.bfloat16)
        return jnp.dot(table, onehot, preferred_element_type=jnp.float32)

    looked = lax.map(lookup, flat_bins)
    looked = jnp.transpose(looked, (1, 0, 2)).reshape(4, depth, rows, cols)
    alpha = looked[3]
    voxels = jnp.concatenate([alpha[None] * shade[None] * looked[0:3], alpha[None]], axis=0)

    def march(step, carry):
        ahead, behind = carry
        near_voxel = lax.dynamic_index_in_dim(voxels, step, 1, keepdims=False)
        far_voxel = lax.dynamic_index_in_dim(voxels, depth - 1 - step, 1, keepdims=False)
        return (stack_over(ahead, near_voxel), stack_over(behind, far_voxel))

    empty = jnp.zeros((4, rows, cols), jnp.float32)
    ahead, behind = lax.fori_loop(0, depth, march, (empty, empty))
    partial_value = jnp.where(view_back == 1, behind, ahead)
    groups = lax.axis_size("gz")
    tile_rows = rows // groups
    tiles = partial_value.reshape(4, groups, tile_rows, cols)
    position = lax.axis_index("gz")
    current = tiles
    for level in range(groups.bit_length() - 1):
        count = current.shape[1]
        halves = current.reshape(4, count // 2, 2, tile_rows, cols)
        lower_half = halves[:, :, 0]
        upper_half = halves[:, :, 1]
        my_bit = position >> level & 1
        kept = jnp.where(my_bit == 0, lower_half, upper_half)
        given = jnp.where(my_bit == 0, upper_half, lower_half)
        received = partner(given, "gz", level)
        nearer = jnp.where(my_bit == 0, kept, received)
        farther = jnp.where(my_bit == 0, received, kept)
        current = depth_pair(nearer, farther, view_back)
    return current.reshape(4, 1, 1, tile_rows, cols)


def solution(mesh):
    return jax.shard_map(
        local,
        mesh=mesh,
        in_specs=(P("gz", "gy", "gx"), P("gz", "gy", "gx"), P(), P(), P("gx")),
        out_specs=P(None, "gy", "gz", None, "gx"),
        check_vma=False,
    )
```

profile of v0, /device:TPU:1, one launch (start us, length us, event | category | flops | bytes accessed | tf_op | source)
XLA Modules:
  0.0 144.8 jit_solution(12283924756278807304)
XLA Ops:
  1.1 4.6 %collective-permute-start = (f32[1,256,256]{2,1,0:T(8,128)S(1)}, f32[1,256,256]{2,1,0:T(8,128)S(1)}, u32[]{:S(2)}, u32[]{:S(2)}) collective-permute-start(f32[1,256,256]{2,1,0:T(8,128)S(1)} %get-tuple-element.224), channel_id=1, source_target_pairs={{0,4},{4,8},{8,12},{12,16},{16,20},{20,24},{24,28},{28,32},{32,36}... | collective-permute-start | bytes 786440 | tf_op jit(solution)/shard_map/ppermute | solution.py:21
  5.7 5.5 %collective-permute-start.1 = (f32[1,256,256]{2,1,0:T(8,128)S(1)}, f32[1,256,256]{2,1,0:T(8,128)S(1)}, u32[]{:S(2)}, u32[]{:S(2)}) collective-permute-start(f32[1,256,256]{2,1,0:T(8,128)S(1)} %get-tuple-element.223), channel_id=1, source_target_pairs={{4,0},{8,4},{12,8},{16,12},{20,16},{24,20},{28,24},{32,28},{36,32}... | collective-permute-start | bytes 786440 | tf_op jit(solution)/shard_map/ppermute | solution.py:23
  12.4 32.5 %while.29 = (s32[]{:T(128)}, f32[16,4,8192]{2,1,0:T(4,128)}, s32[16,8192]{1,0:T(8,128)S(1)}, bf16[4,256]{1,0:T(4,128)(2,1)S(1)}, s32[]{:T(128)}) while((s32[]{:T(128)}, f32[16,4,8192]{2,1,0:T(4,128)}, s32[16,8192]{1,0:T(8,128)S(1)}, bf16[4,256]{1,0:T(4,128)(2,1)S(1)}, s32[]{:T(128)}) %tuple.72), condition=%wide.region_1.2_spmd.clone, body=%wide.region_0.1_spmd.clone.sunk | while | flops 18874368 | bytes 232001 | solution.py:70
  14.5 2.0 %fusion.40 = f32[16,4,8192]{2,1,0:T(4,128)} fusion(f32[16,4,8192]{2,1,0:T(4,128)} %get-tuple-element.289, s32[]{:T(128)} %get-tuple-element.288, bf16[4,256]{1,0:T(4,128)(2,1)S(1)} %get-tuple-element.296, s32[8192]{0:T(1024)S(1)} %bitcast.250), kind=kOutput, calls=%fused_computation.2.clone.1 | convolution fusion | flops 18874368 | bytes 166400 | tf_op jit(solution)/shard_map/while/body/eval_jaxpr/dot_general | solution.py:68
  16.5 2.0 %fusion.40 = f32[16,4,8192]{2,1,0:T(4,128)} fusion(f32[16,4,8192]{2,1,0:T(4,128)} %get-tuple-element.289, s32[]{:T(128)} %get-tuple-element.288, bf16[4,256]{1,0:T(4,128)(2,1)S(1)} %get-tuple-element.296, s32[8192]{0:T(1024)S(1)} %bitcast.250), kind=kOutput, calls=%fused_computation.2.clone.1 | convolution fusion | flops 18874368 | bytes 166400 | tf_op jit(solution)/shard_map/while/body/eval_jaxpr/dot_general | solution.py:68
  18.5 2.0 %fusion.40 = f32[16,4,8192]{2,1,0:T(4,128)} fusion(f32[16,4,8192]{2,1,0:T(4,128)} %get-tuple-element.289, s32[]{:T(128)} %get-tuple-element.288, bf16[4,256]{1,0:T(4,128)(2,1)S(1)} %get-tuple-element.296, s32[8192]{0:T(1024)S(1)} %bitcast.250), kind=kOutput, calls=%fused_computation.2.clone.1 | convolution fusion | flops 18874368 | bytes 166400 | tf_op jit(solution)/shard_map/while/body/eval_jaxpr/dot_general | solution.py:68
  20.6 2.0 %fusion.40 = f32[16,4,8192]{2,1,0:T(4,128)} fusion(f32[16,4,8192]{2,1,0:T(4,128)} %get-tuple-element.289, s32[]{:T(128)} %get-tuple-element.288, bf16[4,256]{1,0:T(4,128)(2,1)S(1)} %get-tuple-element.296, s32[8192]{0:T(1024)S(1)} %bitcast.250), kind=kOutput, calls=%fused_computation.2.clone.1 | convolution fusion | flops 18874368 | bytes 166400 | tf_op jit(solution)/shard_map/while/body/eval_jaxpr/dot_general | solution.py:68
  22.6 2.0 %fusion.40 = f32[16,4,8192]{2,1,0:T(4,128)} fusion(f32[16,4,8192]{2,1,0:T(4,128)} %get-tuple-element.289, s32[]{:T(128)} %get-tuple-element.288, bf16[4,256]{1,0:T(4,128)(2,1)S(1)} %get-tuple-element.296, s32[8192]{0:T(1024)S(1)} %bitcast.250), kind=kOutput, calls=%fused_computation.2.clone.1 | convolution fusion | flops 18874368 | bytes 166400 | tf_op jit(solution)/shard_map/while/body/eval_jaxpr/dot_general | solution.py:68
  24.6 2.0 %fusion.40 = f32[16,4,8192]{2,1,0:T(4,128)} fusion(f32[16,4,8192]{2,1,0:T(4,128)} %get-tuple-element.289, s32[]{:T(128)} %get-tuple-element.288, bf16[4,256]{1,0:T(4,128)(2,1)S(1)} %get-tuple-element.296, s32[8192]{0:T(1024)S(1)} %bitcast.250), kind=kOutput, calls=%fused_computation.2.clone.1 | convolution fusion | flops 18874368 | bytes 166400 | tf_op jit(solution)/shard_map/while/body/eval_jaxpr/dot_general | solution.py:68
  26.6 2.0 %fusion.40 = f32[16,4,8192]{2,1,0:T(4,128)} fusion(f32[16,4,8192]{2,1,0:T(4,128)} %get-tuple-element.289, s32[]{:T(128)} %get-tuple-element.288, bf16[4,256]{1,0:T(4,128)(2,1)S(1)} %get-tuple-element.296, s32[8192]{0:T(1024)S(1)} %bitcast.250), kind=kOutput, calls=%fused_computation.2.clone.1 | convolution fusion | flops 18874368 | bytes 166400 | tf_op jit(solution)/shard_map/while/body/eval_jaxpr/dot_general | solution.py:68
  28.7 2.0 %fusion.40 = f32[16,4,8192]{2,1,0:T(4,128)} fusion(f32[16,4,8192]{2,1,0:T(4,128)} %get-tuple-element.289, s32[]{:T(128)} %get-tuple-element.288, bf16[4,256]{1,0:T(4,128)(2,1)S(1)} %get-tuple-element.296, s32[8192]{0:T(1024)S(1)} %bitcast.250), kind=kOutput, calls=%fused_computation.2.clone.1 | convolution fusion | flops 18874368 | bytes 166400 | tf_op jit(solution)/shard_map/while/body/eval_jaxpr/dot_general | solution.py:68
  30.7 2.0 %fusion.40 = f32[16,4,8192]{2,1,0:T(4,128)} fusion(f32[16,4,8192]{2,1,0:T(4,128)} %get-tuple-element.289, s32[]{:T(128)} %get-tuple-element.288, bf16[4,256]{1,0:T(4,128)(2,1)S(1)} %get-tuple-element.296, s32[8192]{0:T(1024)S(1)} %bitcast.250), kind=kOutput, calls=%fused_computation.2.clone.1 | convolution fusion | flops 18874368 | bytes 166400 | tf_op jit(solution)/shard_map/while/body/eval_jaxpr/dot_general | solution.py:68
  32.7 2.0 %fusion.40 = f32[16,4,8192]{2,1,0:T(4,128)} fusion(f32[16,4,8192]{2,1,0:T(4,128)} %get-tuple-element.289, s32[]{:T(128)} %get-tuple-element.288, bf16[4,256]{1,0:T(4,128)(2,1)S(1)} %get-tuple-element.296, s32[8192]{0:T(1024)S(1)} %bitcast.250), kind=kOutput, calls=%fused_computation.2.clone.1 | convolution fusion | flops 18874368 | bytes 166400 | tf_op jit(solution)/shard_map/while/body/eval_jaxpr/dot_general | solution.py:68
  34.8 2.0 %fusion.40 = f32[16,4,8192]{2,1,0:T(4,128)} fusion(f32[16,4,8192]{2,1,0:T(4,128)} %get-tuple-element.289, s32[]{:T(128)} %get-tuple-element.288, bf16[4,256]{1,0:T(4,128)(2,1)S(1)} %get-tuple-element.296, s32[8192]{0:T(1024)S(1)} %bitcast.250), kind=kOutput, calls=%fused_computation.2.clone.1 | convolution fusion | flops 18874368 | bytes 166400 | tf_op jit(solution)/shard_map/while/body/eval_jaxpr/dot_general | solution.py:68
  36.8 2.0 %fusion.40 = f32[16,4,8192]{2,1,0:T(4,128)} fusion(f32[16,4,8192]{2,1,0:T(4,128)} %get-tuple-element.289, s32[]{:T(128)} %get-tuple-element.288, bf16[4,256]{1,0:T(4,128)(2,1)S(1)} %get-tuple-element.296, s32[8192]{0:T(1024)S(1)} %bitcast.250), kind=kOutput, calls=%fused_computation.2.clone.1 | convolution fusion | flops 18874368 | bytes 166400 | tf_op jit(solution)/shard_map/while/body/eval_jaxpr/dot_general | solution.py:68
  38.8 2.0 %fusion.40 = f32[16,4,8192]{2,1,0:T(4,128)} fusion(f32[16,4,8192]{2,1,0:T(4,128)} %get-tuple-element.289, s32[]{:T(128)} %get-tuple-element.288, bf16[4,256]{1,0:T(4,128)(2,1)S(1)} %get-tuple-element.296, s32[8192]{0:T(1024)S(1)} %bitcast.250), kind=kOutput, calls=%fused_computation.2.clone.1 | convolution fusion | flops 18874368 | bytes 166400 | tf_op jit(solution)/shard_map/while/body/eval_jaxpr/dot_general | solution.py:68
  40.9 2.0 %fusion.40 = f32[16,4,8192]{2,1,0:T(4,128)} fusion(f32[16,4,8192]{2,1,0:T(4,128)} %get-tuple-element.289, s32[]{:T(128)} %get-tuple-element.288, bf16[4,256]{1,0:T(4,128)(2,1)S(1)} %get-tuple-element.296, s32[8192]{0:T(1024)S(1)} %bitcast.250), kind=kOutput, calls=%fused_computation.2.clone.1 | convolution fusion | flops 18874368 | bytes 166400 | tf_op jit(solution)/shard_map/while/body/eval_jaxpr/dot_general | solution.py:68
  42.9 2.0 %fusion.40 = f32[16,4,8192]{2,1,0:T(4,128)} fusion(f32[16,4,8192]{2,1,0:T(4,128)} %get-tuple-element.289, s32[]{:T(128)} %get-tuple-element.288, bf16[4,256]{1,0:T(4,128)(2,1)S(1)} %get-tuple-element.296, s32[8192]{0:T(1024)S(1)} %bitcast.250), kind=kOutput, calls=%fused_computation.2.clone.1 | convolution fusion | flops 18874368 | bytes 166400 | tf_op jit(solution)/shard_map/while/body/eval_jaxpr/dot_general | solution.py:68
  47.6 3.1 %slice_reduce_fusion = f32[16,8192]{1,0:T(8,128)S(1)} fusion(f32[4,16,8192]{2,0,1:T(4,128)} %bitcast.242), kind=kLoop, calls=%fused_computation.34 | loop fusion | bytes 1048576 | tf_op jit(solution)/shard_map/slice | solution.py:72
  56.3 4.0 %collective-permute-start.5 = (f32[4,258,1]{1,0,2:T(4,128)S(1)}, f32[4,258,1]{1,0,2:T(4,128)S(1)}, u32[]{:S(2)}, u32[]{:S(2)}) collective-permute-start(f32[4,258,1]{1,0,2:T(4,128)S(1)} %copy.200), channel_id=1, source_target_pairs={{0,1},{2,3},{4,5},{6,7},{8,9},{10,11},{12,13},{14,15},{16,17},{18,... | collective-permute-start | bytes 12392 | tf_op jit(solution)/shard_map/ppermute | solution.py:21
  62.1 3.6 %copy.202 = f32[3,16,8192]{2,1,0:T(8,128)} copy(f32[3,16,8192]{2,0,1:T(4,128)} %bitcast.243) | data formatting | bytes 3145728 | tf_op jit(solution)/shard_map/slice | solution.py:73
  69.4 2.7 %add_multiply_fusion = f32[2,256,256]{2,1,0:T(8,128)S(1)} fusion(f32[2,256,256]{2,1,0:T(8,128)} %slice.140, f32[2,256,256]{2,1,0:T(8,128)S(1)} %copy-done.1, f32[1,256,256]{2,1,0:T(8,128)S(1)} %collective-permute-done, f32[1,256,256]{2,1,0:T(8,128)} %copy-done.3, f32[4,256,256]{2,1,0:T(8,128)} %copy-done, f32[4,1,256]{2,1,0:T(1,128)S(1)} %collective-permute-done.2, ...), kind=kLoop, calls=%fused_computation.39 | loop fusion | flops 4194304 | bytes 3162176 | tf_op jit(solution)/shard_map/mul | solution.py:73
  73.4 4.3 %while.30 = (s32[]{:T(128)}, f32[4,256,256]{2,1,0:T(8,128)S(1)}, f32[4,256,256]{2,1,0:T(8,128)}, f32[4,2,256,256]{3,2,0,1:T(8,128)S(1)}, s32[]{:T(128)}, /*index=5*/s32[]{:T(128)}, s32[]{:T(128)}) while((s32[]{:T(128)}, f32[4,256,256]{2,1,0:T(8,128)S(1)}, f32[4,256,256]{2,1,0:T(8,128)}, f32[4,2,256,256]{3,2,0,1:T(8,128)S(1)}, ...), condition=%wide.region_3.4_spmd.clone, body=%wide.region_2.3_spmd.clone.sunk | while | flops 1703943 | bytes 12058765 | solution.py:82
  80.0 2.9 %collective-permute-start.6 = (f32[4,64,2,256]{3,2,1,0:T(2,128)S(1)}, f32[4,64,2,256]{3,2,1,0:T(2,128)S(1)}, u32[]{:S(2)}, u32[]{:S(2)}) collective-permute-start(f32[4,64,2,256]{3,2,1,0:T(2,128)S(1)} %select_bitcast_fusion), channel_id=1, source_target_pairs={{0,4},{4,0},{8,12},{12,8},{16,20},{20,16},{24,28},{28,24},{32,36},... | collective-permute-start | bytes 1572872 | tf_op jit(solution)/shard_map/ppermute | solution.py:37
  85.4 4.4 %collective-permute-start.7 = (f32[4,32,2,256]{3,2,1,0:T(2,128)S(1)}, f32[4,32,2,256]{3,2,1,0:T(2,128)S(1)}, u32[]{:S(2)}, u32[]{:S(2)}) collective-permute-start(f32[4,32,2,256]{3,2,1,0:T(2,128)S(1)} %fusion.12), channel_id=1, source_target_pairs={{0,8},{8,0},{4,12},{12,4},{16,24},{24,16},{20,28},{28,20},{32,40},... | collective-permute-start | bytes 786440 | tf_op jit(solution)/shard_map/ppermute | solution.py:37
  89.9 6.4 %collective-permute-done.7 = f32[4,32,2,256]{3,2,1,0:T(2,128)S(1)} collective-permute-done((f32[4,32,2,256]{3,2,1,0:T(2,128)S(1)}, f32[4,32,2,256]{3,2,1,0:T(2,128)S(1)}, u32[]{:S(2)}, u32[]{:S(2)}) %collective-permute-start.7) | collective-permute-done | bytes 262176 | tf_op jit(solution)/shard_map/ppermute | solution.py:37
  96.8 4.1 %collective-permute-start.8 = (f32[4,16,2,256]{3,2,1,0:T(2,128)S(1)}, f32[4,16,2,256]{3,2,1,0:T(2,128)S(1)}, u32[]{:S(2)}, u32[]{:S(2)}) collective-permute-start(f32[4,16,2,256]{3,2,1,0:T(2,128)S(1)} %fusion.15), channel_id=1, source_target_pairs={{0,16},{16,0},{4,20},{20,4},{8,24},{24,8},{12,28},{28,12},{32,48},... | collective-permute-start | bytes 393224 | tf_op jit(solution)/shard_map/ppermute | solution.py:37
  100.9 6.0 %collective-permute-done.8 = f32[4,16,2,256]{3,2,1,0:T(2,128)S(1)} collective-permute-done((f32[4,16,2,256]{3,2,1,0:T(2,128)S(1)}, f32[4,16,2,256]{3,2,1,0:T(2,128)S(1)}, u32[]{:S(2)}, u32[]{:S(2)}) %collective-permute-start.8) | collective-permute-done | bytes 131104 | tf_op jit(solution)/shard_map/ppermute | solution.py:37
  107.2 9.4 %collective-permute-start.9 = (f32[4,8,2,256]{3,2,1,0:T(2,128)S(1)}, f32[4,8,2,256]{3,2,1,0:T(2,128)S(1)}, u32[]{:S(2)}, u32[]{:S(2)}) collective-permute-start(f32[4,8,2,256]{3,2,1,0:T(2,128)S(1)} %fusion.18), channel_id=1, source_target_pairs={{0,32},{32,0},{4,36},{36,4},{8,40},{40,8},{12,44},{44,12},{16,48},... | collective-permute-start | bytes 196616 | tf_op jit(solution)/shard_map/ppermute | solution.py:37
  118.4 4.7 %collective-permute-start.10 = (f32[4,4,2,256]{3,2,1,0:T(2,128)S(1)}, f32[4,4,2,256]{3,2,1,0:T(2,128)S(1)}, u32[]{:S(2)}, u32[]{:S(2)}) collective-permute-start(f32[4,4,2,256]{3,2,1,0:T(2,128)S(1)} %fusion.21), channel_id=1, source_target_pairs={{0,64},{64,0},{4,68},{68,4},{8,72},{72,8},{12,76},{76,12},{16,80},... | collective-permute-start | bytes 98312 | tf_op jit(solution)/shard_map/ppermute | solution.py:37
  124.5 5.8 %collective-permute-start.11 = (f32[4,2,2,256]{3,2,1,0:T(2,128)S(1)}, f32[4,2,2,256]{3,2,1,0:T(2,128)S(1)}, u32[]{:S(2)}, u32[]{:S(2)}) collective-permute-start(f32[4,2,2,256]{3,2,1,0:T(2,128)S(1)} %fusion.24), channel_id=1, source_target_pairs={{0,128},{128,0},{4,132},{132,4},{8,136},{136,8},{12,140},{140,12},... | collective-permute-start | bytes 49160 | tf_op jit(solution)/shard_map/ppermute | solution.py:37
  131.5 11.6 %collective-permute-start.12 = (f32[4,1,2,256]{3,2,0,1:T(2,128)S(1)}, f32[4,1,2,256]{3,2,0,1:T(2,128)S(1)}, u32[]{:S(2)}, u32[]{:S(2)}) collective-permute-start(f32[4,1,2,256]{3,2,0,1:T(2,128)S(1)} %fusion.27), channel_id=1, source_target_pairs={{0,256},{256,0},{4,260},{260,4},{8,264},{264,8},{12,268},{268,12},... | collective-permute-start | bytes 24584 | tf_op jit(solution)/shard_map/ppermute | solution.py:37
  (106 shorter events, 35.3 us)
Async XLA Ops:
  0.0 12.4 %copy-start.4 = (bf16[3,256]{1,0:T(4,128)(2,1)S(1)}, bf16[3,256]{1,0:T(4,128)(2,1)}, u32[]{:S(2)}) copy-start(bf16[3,256]{1,0:T(4,128)(2,1)} %param.11) | copy-start | bytes 4612
  0.0 12.4 %copy-start.5 = (bf16[1,256]{1,0:T(2,128)(2,1)S(1)}, bf16[1,256]{1,0:T(2,128)(2,1)}, u32[]{:S(2)}) copy-start(bf16[1,256]{1,0:T(2,128)(2,1)} %param.12) | copy-start | bytes 1540
  1.1 43.8 %collective-permute-start = (f32[1,256,256]{2,1,0:T(8,128)S(1)}, f32[1,256,256]{2,1,0:T(8,128)S(1)}, u32[]{:S(2)}, u32[]{:S(2)}) collective-permute-start(f32[1,256,256]{2,1,0:T(8,128)S(1)} %get-tuple-element.224), channel_id=1, source_target_pairs={{0,4},{4,8},{8,12},{12,16},{16,20},{20,24},{24,28},{28,32},{32,36}... | collective-permute-start | bytes 786440 | tf_op jit(solution)/shard_map/ppermute | solution.py:21
  5.7 39.3 %collective-permute-start.1 = (f32[1,256,256]{2,1,0:T(8,128)S(1)}, f32[1,256,256]{2,1,0:T(8,128)S(1)}, u32[]{:S(2)}, u32[]{:S(2)}) collective-permute-start(f32[1,256,256]{2,1,0:T(8,128)S(1)} %get-tuple-element.223), channel_id=1, source_target_pairs={{4,0},{8,4},{12,8},{16,12},{20,16},{24,20},{28,24},{32,28},{36,32}... | collective-permute-start | bytes 786440 | tf_op jit(solution)/shard_map/ppermute | solution.py:23
  12.4 32.5 %copy-start.1 = (f32[2,256,256]{2,1,0:T(8,128)S(1)}, f32[2,256,256]{2,1,0:T(8,128)}, u32[]{:S(2)}) copy-start(f32[2,256,256]{2,1,0:T(8,128)} %param.9) | copy-start | bytes 1572868
  45.0 2.7 %copy-start.3 = (f32[1,256,256]{2,1,0:T(8,128)}, f32[1,256,256]{2,1,0:T(8,128)S(1)}, u32[]{:S(2)}) copy-start(f32[1,256,256]{2,1,0:T(8,128)S(1)} %collective-permute-done.1) | copy-start | bytes 786436
  45.0 8.4 %copy-start = (f32[4,256,256]{2,1,0:T(8,128)}, f32[4,256,256]{2,1,0:T(8,128)S(1)}, u32[]{:S(2)}) copy-start(f32[4,256,256]{2,1,0:T(8,128)S(1)} %constant_dynamic-update-slice_fusion) | copy-start | bytes 3145732
  45.0 5.7 %collective-permute-start.2 = (f32[4,1,256]{2,1,0:T(1,128)S(1)}, f32[4,1,256]{2,1,0:T(1,128)S(1)}, u32[]{:S(2)}, u32[]{:S(2)}) collective-permute-start(f32[4,1,256]{2,1,0:T(1,128)S(1)} %get-tuple-element.222), channel_id=1, source_target_pairs={{0,2},{1,3},{4,6},{5,7},{8,10},{9,11},{12,14},{13,15},{16,18},{17,... | collective-permute-start | bytes 12296 | tf_op jit(solution)/shard_map/ppermute | solution.py:21
  46.3 6.0 %collective-permute-start.3 = (f32[4,1,256]{2,1,0:T(1,128)S(1)}, f32[4,1,256]{2,1,0:T(1,128)S(1)}, u32[]{:S(2)}, u32[]{:S(2)}) collective-permute-start(f32[4,1,256]{2,1,0:T(1,128)S(1)} %get-tuple-element.221), channel_id=1, source_target_pairs={{2,0},{3,1},{6,4},{7,5},{10,8},{11,9},{14,12},{15,13},{18,16},{19,... | collective-permute-start | bytes 12296 | tf_op jit(solution)/shard_map/ppermute | solution.py:23
  52.4 7.8 %copy-start.6 = (s32[256]{0:T(256)S(1)}, s32[256]{0:T(256)}, u32[]{:S(2)}) copy-start(s32[256]{0:T(256)} %param.13) | copy-start | bytes 3076
  54.7 12.5 %collective-permute-start.4 = (f32[4,258,1]{1,0,2:T(4,128)S(1)}, f32[4,258,1]{1,0,2:T(4,128)S(1)}, u32[]{:S(2)}, u32[]{:S(2)}) collective-permute-start(f32[4,258,1]{1,0,2:T(4,128)S(1)} %copy.198), channel_id=1, source_target_pairs={{1,0},{3,2},{5,4},{7,6},{9,8},{11,10},{13,12},{15,14},{17,16},{19,... | collective-permute-start | bytes 12392 | tf_op jit(solution)/shard_map/ppermute | solution.py:23
  56.3 12.0 %collective-permute-start.5 = (f32[4,258,1]{1,0,2:T(4,128)S(1)}, f32[4,258,1]{1,0,2:T(4,128)S(1)}, u32[]{:S(2)}, u32[]{:S(2)}) collective-permute-start(f32[4,258,1]{1,0,2:T(4,128)S(1)} %copy.200), channel_id=1, source_target_pairs={{0,1},{2,3},{4,5},{6,7},{8,9},{10,11},{12,13},{14,15},{16,17},{18,... | collective-permute-start | bytes 12392 | tf_op jit(solution)/shard_map/ppermute | solution.py:21
  72.1 1.0 copy-start.2
  80.0 4.4 %collective-permute-start.6 = (f32[4,64,2,256]{3,2,1,0:T(2,128)S(1)}, f32[4,64,2,256]{3,2,1,0:T(2,128)S(1)}, u32[]{:S(2)}, u32[]{:S(2)}) collective-permute-start(f32[4,64,2,256]{3,2,1,0:T(2,128)S(1)} %select_bitcast_fusion), channel_id=1, source_target_pairs={{0,4},{4,0},{8,12},{12,8},{16,20},{20,16},{24,28},{28,24},{32,36},... | collective-permute-start | bytes 1572872 | tf_op jit(solution)/shard_map/ppermute | solution.py:37
  85.4 10.8 %collective-permute-start.7 = (f32[4,32,2,256]{3,2,1,0:T(2,128)S(1)}, f32[4,32,2,256]{3,2,1,0:T(2,128)S(1)}, u32[]{:S(2)}, u32[]{:S(2)}) collective-permute-start(f32[4,32,2,256]{3,2,1,0:T(2,128)S(1)} %fusion.12), channel_id=1, source_target_pairs={{0,8},{8,0},{4,12},{12,4},{16,24},{24,16},{20,28},{28,20},{32,40},... | collective-permute-start | bytes 786440 | tf_op jit(solution)/shard_map/ppermute | solution.py:37
  96.8 10.1 %collective-permute-start.8 = (f32[4,16,2,256]{3,2,1,0:T(2,128)S(1)}, f32[4,16,2,256]{3,2,1,0:T(2,128)S(1)}, u32[]{:S(2)}, u32[]{:S(2)}) collective-permute-start(f32[4,16,2,256]{3,2,1,0:T(2,128)S(1)} %fusion.15), channel_id=1, source_target_pairs={{0,16},{16,0},{4,20},{20,4},{8,24},{24,8},{12,28},{28,12},{32,48},... | collective-permute-start | bytes 393224 | tf_op jit(solution)/shard_map/ppermute | solution.py:37
  107.2 11.0 %collective-permute-start.9 = (f32[4,8,2,256]{3,2,1,0:T(2,128)S(1)}, f32[4,8,2,256]{3,2,1,0:T(2,128)S(1)}, u32[]{:S(2)}, u32[]{:S(2)}) collective-permute-start(f32[4,8,2,256]{3,2,1,0:T(2,128)S(1)} %fusion.18), channel_id=1, source_target_pairs={{0,32},{32,0},{4,36},{36,4},{8,40},{40,8},{12,44},{44,12},{16,48},... | collective-permute-start | bytes 196616 | tf_op jit(solution)/shard_map/ppermute | solution.py:37
  118.4 6.0 %collective-permute-start.10 = (f32[4,4,2,256]{3,2,1,0:T(2,128)S(1)}, f32[4,4,2,256]{3,2,1,0:T(2,128)S(1)}, u32[]{:S(2)}, u32[]{:S(2)}) collective-permute-start(f32[4,4,2,256]{3,2,1,0:T(2,128)S(1)} %fusion.21), channel_id=1, source_target_pairs={{0,64},{64,0},{4,68},{68,4},{8,72},{72,8},{12,76},{76,12},{16,80},... | collective-permute-start | bytes 98312 | tf_op jit(solution)/shard_map/ppermute | solution.py:37
  124.5 6.9 %collective-permute-start.11 = (f32[4,2,2,256]{3,2,1,0:T(2,128)S(1)}, f32[4,2,2,256]{3,2,1,0:T(2,128)S(1)}, u32[]{:S(2)}, u32[]{:S(2)}) collective-permute-start(f32[4,2,2,256]{3,2,1,0:T(2,128)S(1)} %fusion.24), channel_id=1, source_target_pairs={{0,128},{128,0},{4,132},{132,4},{8,136},{136,8},{12,140},{140,12},... | collective-permute-start | bytes 49160 | tf_op jit(solution)/shard_map/ppermute | solution.py:37
  131.5 12.7 %collective-permute-start.12 = (f32[4,1,2,256]{3,2,0,1:T(2,128)S(1)}, f32[4,1,2,256]{3,2,0,1:T(2,128)S(1)}, u32[]{:S(2)}, u32[]{:S(2)}) collective-permute-start(f32[4,1,2,256]{3,2,0,1:T(2,128)S(1)} %fusion.27), channel_id=1, source_target_pairs={{0,256},{256,0},{4,260},{260,4},{8,264},{264,8},{12,268},{268,12},... | collective-permute-start | bytes 24584 | tf_op jit(solution)/shard_map/ppermute | solution.py:37
where the time goes:
time: 147 us; the launch traced here: 145 us
  starting transfers between devices  60.8 us (41%)
  matrix products  32 us (22%)
  waiting for transfers between devices  20.5 us (14%)
  local copies, waits for them, and re-layouts  19.1 us (13%)
  other arithmetic  11.7 us (8%)
    ppermute x7, starting transfers between devices, partner(): return lax.ppermute(block, axis, route)  42.9 us
    dot_general x16, matrix products, lookup(): return jnp.dot(table, onehot, preferred_element_type=jnp.float32)  32 us
    ppermute x7, waiting for transfers between devices, partner(): return lax.ppermute(block, axis, route)  19 us
    ppermute x3, starting transfers between devices, padded_2(): lax.ppermute(tail, axis, [(i, (i + 1) % count) for i in range(ends)])  9.87 us
    ppermute x3, starting transfers between devices, padded_2(): lax.ppermute(head, axis, [((i + 1) % count, i) for i in range(ends)])  8.08 us
    slice x2, local copies, waits for them, and re-layouts, local(): looked[0:3]  5.16 us
    slice x3, local copies, waits for them, and re-layouts, local(): alpha = looked[3]  4.9 us
    add x7, other arithmetic, stack_over(): return front + (1.0 - front[3:4]) * back  3.56 us
  transfers between devices with their start and end apart: 13, of which 8 were waited for; matrix products, arithmetic and copies ran while one was open for 31% of the time, Pallas kernels for 0%

commit v1 on v0

v1 whole, which is shorter than its diff:
```python
import jax
import jax.numpy as jnp
from jax import lax
from jax.experimental import pallas as pl
from jax.experimental.pallas import tpu as pltpu
from jax.sharding import PartitionSpec as P

AMBIENT = 0.2
DIFFUSE = 1.6
LIGHT_X = 0.36
LIGHT_Y = 0.48
LIGHT_Z = 0.8

MESH = pl.DeviceIdType.MESH
NZC = 8
NYC = 8
STEPS = 4


def over(front, front_alpha, back):
    return front + (1.0 - front_alpha) * back


def pair(lower, upper, flip):
    w_lower = jnp.where(flip, 1.0 - upper[3], 1.0)
    w_upper = jnp.where(flip, 1.0, 1.0 - lower[3])
    out = [w_lower * lower[c] + w_upper * upper[c] for c in range(3)]
    out.append(lower[3] + (1.0 - lower[3]) * upper[3])
    return out


def kernel(
    density, bins, color, opacity, view, out,
    dens, bin_v, coef, zh, xh, xsend, xrecv, part, drecv, ysend, yrecv, zsend, zrecv,
    in_sem, zh_s, zh_r, x_s, x_r, yh_s, yh_r, d_s, d_r, y_s, y_r, z_s, z_r,
):
    g = lax.axis_index("gz")
    gy = lax.axis_index("gy")
    gx = lax.axis_index("gx")
    z = lax.div(g, 16)
    y = lax.rem(lax.div(g, 2), 8)
    k = lax.rem(g, 2)
    g_prev = lax.rem(g + 127, 128)
    g_next = lax.rem(g + 1, 128)
    sibling = g + 1 - 2 * k

    def at(zz, yy, kk):
        return ((zz * 8 + yy) * 2 + kk, gy, gx)

    barrier = pltpu.get_barrier_semaphore()

    def greet(target):
        pl.semaphore_signal(barrier, inc=1, device_id=target, device_id_type=MESH)

    greet((g_prev, gy, gx))
    greet((g_next, gy, gx))
    greet((g, gy, 1 - gx))
    greet((g, 1 - gy, gx))
    for j in range(1, 8):
        greet(at(z, lax.rem(y + j, 8), k))
        greet(at(lax.rem(z + j, 8), y, 0))
        greet(at(lax.rem(z + j, 8), y, 1))

    load_d = pltpu.make_async_copy(density, dens.at[:, pl.ds(8, 256), :], in_sem.at[0])
    load_b = pltpu.make_async_copy(bins, bin_v, in_sem.at[1])
    load_d.start()
    load_b.start()

    zero_row = pl.multiple_of(gy * 264, 8)
    dens[:, pl.ds(zero_row, 8), :] = jnp.zeros((2, 8, 256), jnp.float32)

    lane = lax.broadcasted_iota(jnp.int32, (8, 128), 1)
    sub = lax.broadcasted_iota(jnp.int32, (8, 128), 0)

    view_rows = view[...].reshape(1, 256)
    flips = [jnp.broadcast_to(view_rows[:, 128 * h:128 * h + 128], (8, 128)) == 1 for h in range(2)]

    load_d.wait()
    edge = pl.multiple_of((1 - gx) * 128, 128)
    packed = jnp.zeros((8, 128), jnp.float32)
    for layer in range(2):
        for t in range(32):
            i = layer * 32 + t
            tile = dens[layer, pl.ds(8 + 8 * t, 8), pl.ds(edge, 128)]
            tile = jnp.where(gx == 0, pltpu.roll(tile, i + 1, 1), pltpu.roll(tile, i, 1))
            packed = jnp.where(lane == i, tile, packed)
    xsend[...] = packed

    def owner_a(zz, s):
        return lax.rem(zz + 4 + s, 8)

    def owner_b(zz, s):
        return lax.rem(zz + 11 - s, 8)

    load_b.wait()
    tables = jnp.concatenate([color[...].astype(jnp.float32), opacity[...].astype(jnp.float32)], axis=0)
    table = [[jnp.broadcast_to(tables[c:c + 1, 128 * h:128 * h + 128], (8, 128)) for h in range(2)] for c in range(4)]

    def look(entry):
        low = jnp.bitwise_and(entry, 127)
        high = entry >= 128
        return [
            jnp.where(
                high,
                jnp.take_along_axis(table[c][1], low, axis=1, mode="promise_in_bounds"),
                jnp.take_along_axis(table[c][0], low, axis=1, mode="promise_in_bounds"),
            )
            for c in range(4)
        ]

    def lookup_block(j, carry):
        s = lax.div(j, 2)
        ab = lax.rem(j, 2)
        zb = jnp.where(ab == 0, owner_a(z, s), owner_b(z, s))
        for m in range(4):
            row = pl.multiple_of(32 * zb + 8 * m, 8)
            for h in range(2):
                cols = pl.ds(128 * h, 128)
                near = look(bin_v[0, pl.ds(row, 8), cols])
                far = look(bin_v[1, pl.ds(row, 8), cols])
                k_near = jnp.where(flips[h], 1.0 - far[3], 1.0) * near[3]
                k_far = jnp.where(flips[h], 1.0, 1.0 - near[3]) * far[3]
                for c in range(3):
                    coef[c, pl.ds(row, 8), cols] = k_near * near[c]
                    coef[3 + c, pl.ds(row, 8), cols] = k_far * far[c]
                part[s, h, 3, ab, pl.ds(8 * m, 8), :] = near[3] + (1.0 - near[3]) * far[3]
        return carry

    lax.fori_loop(0, 8, lookup_block, 0)

    pl.semaphore_wait(barrier, 25)

    x_copy = pltpu.make_async_remote_copy(
        src_ref=xsend, dst_ref=xrecv, send_sem=x_s, recv_sem=x_r,
        device_id=(g, gy, 1 - gx), device_id_type=MESH)
    x_copy.start()
    y_from = pl.multiple_of(jnp.where(gy == 0, 256, 8), 8)
    y_to = pl.multiple_of(jnp.where(gy == 0, 0, 264), 8)
    yh_copy = pltpu.make_async_remote_copy(
        src_ref=dens.at[:, pl.ds(y_from, 8), :], dst_ref=dens.at[:, pl.ds(y_to, 8), :],
        send_sem=yh_s, recv_sem=yh_r, device_id=(g, 1 - gy, gx), device_id_type=MESH)
    yh_copy.start()

    def z_copy(up, j):
        target = g_next if up else g_prev
        tz = lax.div(target, 16)
        s = lax.div(j, 2)
        zb = jnp.where(lax.rem(j, 2) == 0, owner_a(tz, s), owner_b(tz, s))
        row = pl.multiple_of(32 * zb, 32)
        slot = 0 if up else 1
        return pltpu.make_async_remote_copy(
            src_ref=dens.at[1 if up else 0, pl.ds(8 + row, 32), :],
            dst_ref=zh.at[slot, pl.ds(row, 32), :],
            send_sem=zh_s.at[slot, j], recv_sem=zh_r.at[slot, j],
            device_id=(target, gy, gx), device_id_type=MESH)

    def z_start(j, carry):
        z_copy(True, j).start()
        z_copy(False, j).start()
        return carry

    lax.fori_loop(0, 8, z_start, 0)

    x_copy.wait_recv()
    columns = xrecv[...]
    for layer in range(2):
        for t in range(32):
            i = layer * 32 + t
            xh[layer, pl.ds(8 * t, 8), :] = jnp.broadcast_to(columns[:, i:i + 1], (8, 128))
    yh_copy.wait_recv()

    def shade_block(j, carry):
        s = lax.div(j, 2)
        ab = lax.rem(j, 2)
        zb = jnp.where(ab == 0, owner_a(z, s), owner_b(z, s))
        base = pl.multiple_of(32 * zb, 32)
        for slot in range(2):
            pltpu.make_async_copy(
                zh.at[slot, pl.ds(base, 32), :], zh.at[slot, pl.ds(base, 32), :], zh_r.at[slot, j]).wait()
        first = g == 0
        last = g == 127
        tiles = [[[dens[layer, pl.ds(pl.multiple_of(base + 8 * t, 8), 8), pl.ds(128 * h, 128)] for h in range(2)]
                  for t in range(6)] for layer in range(2)]
        for m in range(4):
            row = pl.multiple_of(base + 8 * m, 8)
            shades = []
            for layer in range(2):
                before, here, after = tiles[layer][m], tiles[layer][m + 1], tiles[layer][m + 2]
                side = xh[layer, pl.ds(row, 8), :]
                ends = [jnp.where(gx == 1, side, 0.0), jnp.where(gx == 0, side, 0.0)]
                to_right = [pltpu.roll(here[h], 1, 1) for h in range(2)]
                to_left = [pltpu.roll(here[h], 127, 1) for h in range(2)]
                left = [jnp.where(lane == 0, ends[0], to_right[0]), jnp.where(lane == 0, to_right[0], to_right[1])]
                right = [jnp.where(lane == 127, to_left[1], to_left[0]), jnp.where(lane == 127, ends[1], to_left[1])]
                for h in range(2):
                    cols = pl.ds(128 * h, 128)
                    above = jnp.where(sub == 0, pltpu.roll(before[h], 1, 0), pltpu.roll(here[h], 1, 0))
                    below = jnp.where(sub == 7, pltpu.roll(after[h], 7, 0), pltpu.roll(here[h], 7, 0))
                    other = tiles[1 - layer][m + 1][h]
                    if layer == 0:
                        dz = other - jnp.where(first, 0.0, zh[0, pl.ds(row, 8), cols])
                    else:
                        dz = jnp.where(last, 0.0, zh[1, pl.ds(row, 8), cols]) - other
                    dx = right[h] - left[h]
                    dy = below - above
                    dot = dx * (0.5 * DIFFUSE * LIGHT_X) + dy * (0.5 * DIFFUSE * LIGHT_Y) + dz * (0.5 * DIFFUSE * LIGHT_Z)
                    norm = 1.0 + 0.25 * (dx * dx + dy * dy + dz * dz)
                    shades.append(AMBIENT + jnp.abs(dot) * lax.rsqrt(norm))
            for h in range(2):
                cols = pl.ds(128 * h, 128)
                for c in range(3):
                    part[s, h, c, ab, pl.ds(8 * m, 8), :] = (
                        coef[c, pl.ds(row, 8), cols] * shades[h] + coef[3 + c, pl.ds(row, 8), cols] * shades[2 + h])
        return carry

    def d_copy(s):
        return pltpu.make_async_remote_copy(
            src_ref=part.at[s, 1 - k], dst_ref=drecv.at[s], send_sem=d_s.at[s], recv_sem=d_r.at[s],
            device_id=(sibling, gy, gx), device_id_type=MESH)

    flip = jnp.where(k == 0, flips[0].astype(jnp.int32), flips[1].astype(jnp.int32)) == 1
    own_front = jnp.where(flip, 1, 0) == k

    def y_copy(s, j):
        yy = lax.rem(y + j, 8)
        return pltpu.make_async_remote_copy(
            src_ref=ysend.at[s, yy], dst_ref=yrecv.at[s, y], send_sem=y_s.at[s], recv_sem=y_r.at[s],
            device_id=at(z, yy, k), device_id_type=MESH)

    def merge_pack(s):
        d_copy(s).wait_recv()
        for m in range(4):
            rows = pl.ds(8 * m, 8)
            merged = []
            for ab in range(2):
                own = [part[s, k, c, ab, rows, :] for c in range(4)]
                sib = [drecv[s, c, ab, rows, :] for c in range(4)]
                front = [jnp.where(own_front, own[c], sib[c]) for c in range(4)]
                back = [jnp.where(own_front, sib[c], own[c]) for c in range(4)]
                merged.append([over(front[c], front[3], back[c]) for c in range(4)])
            for c in range(4):
                a, b = merged[0][c], merged[1][c]
                ysend[s, 2 * m, c] = jnp.where(sub < 4, a, pltpu.roll(b, 4, 0))
                ysend[s, 2 * m + 1, c] = jnp.where(sub < 4, pltpu.roll(a, 4, 0), b)
        yrecv[s, y] = ysend[s, y]
        for j in (4, 3, 5, 2, 6, 1, 7):
            y_copy(s, j).start()

    def step(s, carry):
        lax.fori_loop(2 * s, 2 * s + 2, shade_block, 0)
        d_copy(s).start()

        @pl.when(s >= 1)
        def _():
            merge_pack(s - 1)
        return carry

    lax.fori_loop(0, STEPS, step, 0)
    merge_pack(STEPS - 1)

    def z_target(s, ab):
        return owner_a(z, s) if ab == 0 else owner_b(z, s)

    def z_send(s, carry):
        pltpu.make_async_copy(yrecv.at[s, pl.ds(0, 7)], yrecv.at[s, pl.ds(0, 7)], y_r.at[s]).wait()
        level = [[yrecv[s, i, c] for c in range(4)] for i in range(8)]
        while len(level) > 1:
            level = [pair(level[i], level[i + 1], flip) for i in range(0, len(level), 2)]
        total = level[0]
        for ab in range(2):
            for kk in range(2):
                d = 2 * ab + kk
                piece = pltpu.roll(total[0], (8 - 2 * d) % 8, 0) if d else total[0]
                for c in range(1, 4):
                    shift = (2 * c - 2 * d) % 8
                    moved = pltpu.roll(total[c], shift, 0) if shift else total[c]
                    piece = jnp.where(sub < 2 * c, piece, moved)
                zsend[s, ab, kk] = piece
                zt = z_target(s, ab)
                mine = jnp.logical_and(zt == z, k == kk)

                @pl.when(mine)
                def _():
                    zrecv[2 * z + k] = piece

                @pl.when(jnp.logical_not(mine))
                def _():
                    pltpu.make_async_remote_copy(
                        src_ref=zsend.at[s, ab, kk], dst_ref=zrecv.at[2 * z + k], send_sem=z_s, recv_sem=z_r,
                        device_id=at(zt, y, kk), device_id_type=MESH).start()
        return carry

    lax.fori_loop(0, STEPS, z_send, 0)

    pltpu.make_async_copy(zrecv.at[pl.ds(0, 15)], zrecv.at[pl.ds(0, 15)], z_r).wait()
    for h in range(2):
        level = []
        for i in range(8):
            value = zrecv[2 * i + h]
            spread = jnp.where(sub >= 6, value, pltpu.roll(value, 6, 0))
            spread = jnp.where(sub >= 4, spread, pltpu.roll(spread, 4, 0))
            level.append((value, spread))
        while len(level) > 1:
            merged = []
            for i in range(0, len(level), 2):
                (lv, la), (uv, ua) = level[i], level[i + 1]
                fv, fa = jnp.where(flips[h], uv, lv), jnp.where(flips[h], ua, la)
                bv, ba = jnp.where(flips[h], lv, uv), jnp.where(flips[h], la, ua)
                merged.append((over(fv, fa, bv), over(fa, fa, ba)))
            level = merged
        for c in range(4):
            out[c, :, pl.ds(128 * h, 128)] = level[0][0][2 * c:2 * c + 2, :]

    x_copy.wait_send()
    yh_copy.wait_send()

    def z_drain(j, carry):
        z_copy(True, j).wait_send()
        z_copy(False, j).wait_send()
        return carry

    lax.fori_loop(0, 8, z_drain, 0)

    def s_drain(s, carry):
        d_copy(s).wait_send()
        pltpu.make_async_copy(ysend.at[s, pl.ds(0, 7)], ysend.at[s, pl.ds(0, 7)], y_s.at[s]).wait()
        return carry

    lax.fori_loop(0, STEPS, s_drain, 0)
    pltpu.make_async_copy(zrecv.at[pl.ds(0, 15)], zrecv.at[pl.ds(0, 15)], z_s).wait()


def local(density, bins, tf_color, tf_opacity, view_back):
    f32 = jnp.float32
    vmem = pl.BlockSpec(memory_space=pltpu.VMEM)
    anyspace = pl.BlockSpec(memory_space=pl.ANY)
    dma = pltpu.SemaphoreType.DMA
    result = pl.pallas_call(
        kernel,
        out_shape=jax.ShapeDtypeStruct((4, 2, 256), f32),
        in_specs=[anyspace, anyspace, vmem, vmem, vmem],
        out_specs=vmem,
        scratch_shapes=[
            pltpu.VMEM((2, 272, 256), f32),
            pltpu.VMEM((2, 256, 256), jnp.int32),
            pltpu.VMEM((6, 256, 256), f32),
            pltpu.VMEM((2, 256, 256), f32),
            pltpu.VMEM((2, 256, 128), f32),
            pltpu.VMEM((8, 128), f32),
            pltpu.VMEM((8, 128), f32),
            pltpu.VMEM((STEPS, 2, 4, 2, 32, 128), f32),
            pltpu.VMEM((STEPS, 4, 2, 32, 128), f32),
            pltpu.VMEM((STEPS, 8, 4, 8, 128), f32),
            pltpu.VMEM((STEPS, 8, 4, 8, 128), f32),
            pltpu.VMEM((STEPS, 2, 2, 8, 128), f32),
            pltpu.VMEM((16, 8, 128), f32),
            dma((2,)),
            dma((2, 8)),
            dma((2, 8)),
            dma, dma, dma, dma,
            dma((STEPS,)),
            dma((STEPS,)),
            dma((STEPS,)),
            dma((STEPS,)),
            dma, dma,
        ],
        compiler_params=pltpu.CompilerParams(
            collective_id=0, has_side_effects=True, vmem_limit_bytes=32 << 20),
    )(density, bins, tf_color, tf_opacity, view_back)
    return result.reshape(4, 1, 1, 2, 256)


def solution(mesh):
    return jax.shard_map(
        local,
        mesh=mesh,
        in_specs=(P("gz", "gy", "gx"), P("gz", "gy", "gx"), P(), P(), P("gx")),
        out_specs=P(None, "gy", "gz", None, "gx"),
        check_vma=False,
    )
```

time: 147 us -> 41.8 us (0.28); the launches traced: 145 us -> 41.6 us
  starting transfers between devices: 60.8 us -> 0 us
  Pallas kernels: 0 us -> 36.8 us
  matrix products: 32 us -> 0 us
  waiting for transfers between devices: 20.5 us -> 0 us
  local copies, waits for them, and re-layouts: 19.1 us -> 4.72 us
  other arithmetic: 11.7 us -> 0 us
    ppermute x13 -> x0, starting transfers between devices: 60.8 us -> none  [the longest x7 42.9 us: partner(): return lax.ppermute(block, axis, route)]
    pallas_call x0 -> x1, Pallas kernels: none -> 36.8 us  [local(): pl.pallas_call(kernel, out_shape=jax.ShapeDtypeStruct((4, 2, 256), f32),...]
    dot_general x16 -> x0, matrix products: 32 us -> none  [lookup(): return jnp.dot(table, onehot, preferred_element_type=jnp.float32)]
    ppermute x13 -> x0, waiting for transfers between devices: 20.5 us -> none  [the longest x7 19 us: partner(): return lax.ppermute(block, axis, route)]
    slice x10 -> x0, local copies, waits for them, and re-layouts: 13.7 us -> none  [the longest x2 5.16 us: local(): looked[0:3]]
    unnamed x17 -> x11, local copies, waits for them, and re-layouts: 1.11 us -> 4.72 us
    add x7 -> x0, other arithmetic: 3.56 us -> none  [stack_over(): return front + (1.0 - front[3:4]) * back]
    mul x13 -> x0, other arithmetic: 3.07 us -> none  [the longest x2 2.86 us: local(): alpha[None] * shade[None] * looked[0:3]]
  transfers between devices with their start and end apart: 13 -> 0, of which waited for: 8 -> 0; matrix products, arithmetic and copies ran while one was open for 31% -> 0% of each run, Pallas kernels for 0% -> 0%
where the time goes in v1:
time: 41.8 us; the launch traced here: 41.6 us
  Pallas kernels  36.8 us (88%)
  local copies, waits for them, and re-layouts  4.72 us (11%)
    pallas_call x1, Pallas kernels, local(): pl.pallas_call(kernel, out_shape=jax.ShapeDtypeStruct((4, 2, 256), f32),...  36.8 us
    unnamed x11, local copies, waits for them, and re-layouts  4.72 us

profile of v1, /device:TPU:1, one launch (start us, length us, event | category | flops | bytes accessed | tf_op | source)
XLA Modules:
  0.0 41.6 jit_solution(3665228533521587011)
XLA Ops:
  0.0 0.0 copy-start
  0.0 1.0 %copy-done = f32[2,256,256]{2,1,0:T(8,128)S(1)} copy-done((f32[2,256,256]{2,1,0:T(8,128)S(1)}, f32[2,256,256]{2,1,0:T(8,128)}, u32[]{:S(2)}) %copy-start) | copy-done | bytes 524312
  1.0 0.0 copy-start.1
  1.0 1.0 %copy-done.1 = s32[2,256,256]{2,1,0:T(8,128)S(1)} copy-done((s32[2,256,256]{2,1,0:T(8,128)S(1)}, s32[2,256,256]{2,1,0:T(8,128)}, u32[]{:S(2)}) %copy-start.1) | copy-done | bytes 524312
  2.1 0.0 copy-start.2
  2.1 0.7 %copy-done.2 = bf16[3,256]{1,0:T(4,128)(2,1)S(1)} copy-done((bf16[3,256]{1,0:T(4,128)(2,1)S(1)}, bf16[3,256]{1,0:T(4,128)(2,1)}, u32[]{:S(2)}) %copy-start.2) | copy-done | bytes 1560
  2.8 0.0 copy-start.3
  2.8 0.7 %copy-done.3 = bf16[1,256]{1,0:T(2,128)(2,1)S(1)} copy-done((bf16[1,256]{1,0:T(2,128)(2,1)S(1)}, bf16[1,256]{1,0:T(2,128)(2,1)}, u32[]{:S(2)}) %copy-start.3) | copy-done | bytes 536
  3.4 0.0 copy-start.4
  3.4 0.7 %copy-done.4 = s32[256]{0:T(256)S(1)} copy-done((s32[256]{0:T(256)S(1)}, s32[256]{0:T(256)}, u32[]{:S(2)}) %copy-start.4) | copy-done | bytes 1048
  4.1 36.8 %shard_map.55 = f32[4,2,256]{2,1,0:T(2,128)S(1)} custom-call(f32[2,256,256]{2,1,0:T(8,128)S(1)} %copy-done, s32[2,256,256]{2,1,0:T(8,128)S(1)} %copy-done.1, bf16[3,256]{1,0:T(4,128)(2,1)S(1)} %copy-done.2, bf16[1,256]{1,0:T(2,128)(2,1)S(1)} %copy-done.3, s32[256]{0:T(256)S(1)} %copy-done.4), custom_call_target="tpu_custom_call" | custom-call | tf_op jit(solution)/shard_map/pallas_call | solution.py:338
  41.0 0.6 %copy.8 = f32[4,1,1,2,256]{4,3,2,1,0:T(2,128)} copy(f32[4,1,1,2,256]{4,3,2,1,0:T(2,128)S(1)} %bitcast.3) | data formatting | bytes 16384
Async XLA Ops:
  0.0 1.0 %copy-start = (f32[2,256,256]{2,1,0:T(8,128)S(1)}, f32[2,256,256]{2,1,0:T(8,128)}, u32[]{:S(2)}) copy-start(f32[2,256,256]{2,1,0:T(8,128)} %density.1) | copy-start | bytes 1572868
  1.0 1.0 %copy-start.1 = (s32[2,256,256]{2,1,0:T(8,128)S(1)}, s32[2,256,256]{2,1,0:T(8,128)}, u32[]{:S(2)}) copy-start(s32[2,256,256]{2,1,0:T(8,128)} %bins.1) | copy-start | bytes 1572868
  2.1 0.7 %copy-start.2 = (bf16[3,256]{1,0:T(4,128)(2,1)S(1)}, bf16[3,256]{1,0:T(4,128)(2,1)}, u32[]{:S(2)}) copy-start(bf16[3,256]{1,0:T(4,128)(2,1)} %color.1) | copy-start | bytes 4612
  2.8 0.7 %copy-start.3 = (bf16[1,256]{1,0:T(2,128)(2,1)S(1)}, bf16[1,256]{1,0:T(2,128)(2,1)}, u32[]{:S(2)}) copy-start(bf16[1,256]{1,0:T(2,128)(2,1)} %opacity.1) | copy-start | bytes 1540
  3.4 0.7 %copy-start.4 = (s32[256]{0:T(256)S(1)}, s32[256]{0:T(256)}, u32[]{:S(2)}) copy-start(s32[256]{0:T(256)} %view.1) | copy-start | bytes 3076

commit v2 on v1

--- a/solution.py
+++ b/solution.py
@@ -12,27 +12,19 @@
 LIGHT_Z = 0.8
 
 MESH = pl.DeviceIdType.MESH
-NZC = 8
-NYC = 8
-STEPS = 4
+STEPS = 8
+LAG = 4
+Y_ORDER = (0, 1, 7, 2, 6, 3, 5, 4)
 
 
 def over(front, front_alpha, back):
     return front + (1.0 - front_alpha) * back
 
 
-def pair(lower, upper, flip):
-    w_lower = jnp.where(flip, 1.0 - upper[3], 1.0)
-    w_upper = jnp.where(flip, 1.0, 1.0 - lower[3])
-    out = [w_lower * lower[c] + w_upper * upper[c] for c in range(3)]
-    out.append(lower[3] + (1.0 - lower[3]) * upper[3])
-    return out
-
-
 def kernel(
-    density, bins, color, opacity, view, out,
-    dens, bin_v, coef, zh, xh, xsend, xrecv, part, drecv, ysend, yrecv, zsend, zrecv,
-    in_sem, zh_s, zh_r, x_s, x_r, yh_s, yh_r, d_s, d_r, y_s, y_r, z_s, z_r,
+    density, bins, color_h, opacity_h, view_h, out,
+    color, opacity, view, dens, bin_v, coef, zh, xh, xsend, xrecv, part, drecv, ysend, yrecv, zsend, zrecv,
+    in_sem, zh_s, zh_r, x_s, x_r, yh_s, yh_r, d_s, d_r, y_s, y_r, z_s, z_r, y_ready, z_ready,
 ):
     g = lax.axis_index("gz")
     gy = lax.axis_index("gy")
@@ -52,11 +44,11 @@
     def greet(target):
         pl.semaphore_signal(barrier, inc=1, device_id=target, device_id_type=MESH)
 
+    greet((g, 1 - gy, gx))
     greet((g_prev, gy, gx))
     greet((g_next, gy, gx))
     greet((g, gy, 1 - gx))
-    greet((g, 1 - gy, gx))
-    for j in range(1, 8):
+    for j in (1, 7, 2, 6):
         greet(at(z, lax.rem(y + j, 8), k))
         greet(at(lax.rem(z + j, 8), y, 0))
         greet(at(lax.rem(z + j, 8), y, 1))
@@ -65,6 +57,12 @@
     load_b = pltpu.make_async_copy(bins, bin_v, in_sem.at[1])
     load_d.start()
     load_b.start()
+    loads = [
+        pltpu.make_async_copy(src, dst, in_sem.at[2 + i])
+        for i, (src, dst) in enumerate(((color_h, color), (opacity_h, opacity), (view_h, view)))
+    ]
+    for copy in loads:
+        copy.start()
 
     zero_row = pl.multiple_of(gy * 264, 8)
     dens[:, pl.ds(zero_row, 8), :] = jnp.zeros((2, 8, 256), jnp.float32)
@@ -72,6 +70,8 @@
     lane = lax.broadcasted_iota(jnp.int32, (8, 128), 1)
     sub = lax.broadcasted_iota(jnp.int32, (8, 128), 0)
 
+    for copy in loads:
+        copy.wait()
     view_rows = view[...].reshape(1, 256)
     flips = [jnp.broadcast_to(view_rows[:, 128 * h:128 * h + 128], (8, 128)) == 1 for h in range(2)]
 
@@ -85,12 +85,6 @@
             tile = jnp.where(gx == 0, pltpu.roll(tile, i + 1, 1), pltpu.roll(tile, i, 1))
             packed = jnp.where(lane == i, tile, packed)
     xsend[...] = packed
-
-    def owner_a(zz, s):
-        return lax.rem(zz + 4 + s, 8)
-
-    def owner_b(zz, s):
-        return lax.rem(zz + 11 - s, 8)
 
     load_b.wait()
     tables = jnp.concatenate([color[...].astype(jnp.float32), opacity[...].astype(jnp.float32)], axis=0)
@@ -108,12 +102,9 @@
             for c in range(4)
         ]
 
-    def lookup_block(j, carry):
-        s = lax.div(j, 2)
-        ab = lax.rem(j, 2)
-        zb = jnp.where(ab == 0, owner_a(z, s), owner_b(z, s))
+    def lookup_block(s, carry):
         for m in range(4):
-            row = pl.multiple_of(32 * zb + 8 * m, 8)
+            row = pl.multiple_of(32 * s + 8 * m, 8)
             for h in range(2):
                 cols = pl.ds(128 * h, 128)
                 near = look(bin_v[0, pl.ds(row, 8), cols])
@@ -123,12 +114,12 @@
                 for c in range(3):
                     coef[c, pl.ds(row, 8), cols] = k_near * near[c]
                     coef[3 + c, pl.ds(row, 8), cols] = k_far * far[c]
-                part[s, h, 3, ab, pl.ds(8 * m, 8), :] = near[3] + (1.0 - near[3]) * far[3]
+                part[s, h, 3, pl.ds(8 * m, 8), :] = near[3] + (1.0 - near[3]) * far[3]
         return carry
 
     lax.fori_loop(0, 8, lookup_block, 0)
 
-    pl.semaphore_wait(barrier, 25)
+    pl.semaphore_wait(barrier, 16)
 
     x_copy = pltpu.make_async_remote_copy(
         src_ref=xsend, dst_ref=xrecv, send_sem=x_s, recv_sem=x_r,
@@ -143,10 +134,7 @@
 
     def z_copy(up, j):
         target = g_next if up else g_prev
-        tz = lax.div(target, 16)
-        s = lax.div(j, 2)
-        zb = jnp.where(lax.rem(j, 2) == 0, owner_a(tz, s), owner_b(tz, s))
-        row = pl.multiple_of(32 * zb, 32)
+        row = pl.multiple_of(32 * j, 32)
         slot = 0 if up else 1
         return pltpu.make_async_remote_copy(
             src_ref=dens.at[1 if up else 0, pl.ds(8 + row, 32), :],
@@ -160,6 +148,12 @@
         return carry
 
     lax.fori_loop(0, 8, z_start, 0)
+
+    for j in (2, 6):
+        pl.semaphore_signal(y_ready, inc=1, device_id=at(z, lax.rem(y + j, 8), k), device_id_type=MESH)
+    for j in (2, 6):
+        for kk in range(2):
+            pl.semaphore_signal(z_ready, inc=1, device_id=at(lax.rem(z + j, 8), y, kk), device_id_type=MESH)
 
     x_copy.wait_recv()
     columns = xrecv[...]
@@ -169,14 +163,11 @@
             xh[layer, pl.ds(8 * t, 8), :] = jnp.broadcast_to(columns[:, i:i + 1], (8, 128))
     yh_copy.wait_recv()
 
-    def shade_block(j, carry):
-        s = lax.div(j, 2)
-        ab = lax.rem(j, 2)
-        zb = jnp.where(ab == 0, owner_a(z, s), owner_b(z, s))
-        base = pl.multiple_of(32 * zb, 32)
+    def shade_block(s):
+        base = pl.multiple_of(32 * s, 32)
         for slot in range(2):
             pltpu.make_async_copy(
-                zh.at[slot, pl.ds(base, 32), :], zh.at[slot, pl.ds(base, 32), :], zh_r.at[slot, j]).wait()
+                zh.at[slot, pl.ds(base, 32), :], zh.at[slot, pl.ds(base, 32), :], zh_r.at[slot, s]).wait()
         first = g == 0
         last = g == 127
         tiles = [[[dens[layer, pl.ds(pl.multiple_of(base + 8 * t, 8), 8), pl.ds(128 * h, 128)] for h in range(2)]
@@ -209,9 +200,8 @@
             for h in range(2):
                 cols = pl.ds(128 * h, 128)
                 for c in range(3):
-                    part[s, h, c, ab, pl.ds(8 * m, 8), :] = (
+                    part[s, h, c, pl.ds(8 * m, 8), :] = (
                         coef[c, pl.ds(row, 8), cols] * shades[h] + coef[3 + c, pl.ds(row, 8), cols] * shades[2 + h])
-        return carry
 
     def d_copy(s):
         return pltpu.make_async_remote_copy(
@@ -221,8 +211,7 @@
     flip = jnp.where(k == 0, flips[0].astype(jnp.int32), flips[1].astype(jnp.int32)) == 1
     own_front = jnp.where(flip, 1, 0) == k
 
-    def y_copy(s, j):
-        yy = lax.rem(y + j, 8)
+    def y_copy(s, yy):
         return pltpu.make_async_remote_copy(
             src_ref=ysend.at[s, yy], dst_ref=yrecv.at[s, y], send_sem=y_s.at[s], recv_sem=y_r.at[s],
             device_id=at(z, yy, k), device_id_type=MESH)
@@ -231,66 +220,79 @@
         d_copy(s).wait_recv()
         for m in range(4):
             rows = pl.ds(8 * m, 8)
+            own = [part[s, k, c, rows, :] for c in range(4)]
+            sib = [drecv[s, c, rows, :] for c in range(4)]
+            front = [jnp.where(own_front, own[c], sib[c]) for c in range(4)]
+            back = [jnp.where(own_front, sib[c], own[c]) for c in range(4)]
+            merged = [over(front[c], front[3], back[c]) for c in range(4)]
+            turned = [pltpu.roll(merged[c], 4, 0) for c in range(4)]
+            for c in range(2):
+                ysend[s, 2 * m, c] = jnp.where(sub < 4, merged[2 * c], turned[2 * c + 1])
+                ysend[s, 2 * m + 1, c] = jnp.where(sub < 4, turned[2 * c], merged[2 * c + 1])
+        yrecv[s, y] = ysend[s, y]
+        for yy in Y_ORDER:
+            @pl.when(yy != y)
+            def _():
+                y_copy(s, yy).start()
+
+    def z_send(s):
+        pltpu.make_async_copy(yrecv.at[s, pl.ds(0, 7)], yrecv.at[s, pl.ds(0, 7)], y_r.at[s]).wait()
+        level = []
+        for i in range(8):
+            rg, ba = yrecv[s, i, 0], yrecv[s, i, 1]
+            level.append((rg, ba, jnp.where(sub < 4, pltpu.roll(ba, 4, 0), ba)))
+        while len(level) > 1:
             merged = []
-            for ab in range(2):
-                own = [part[s, k, c, ab, rows, :] for c in range(4)]
-                sib = [drecv[s, c, ab, rows, :] for c in range(4)]
-                front = [jnp.where(own_front, own[c], sib[c]) for c in range(4)]
-                back = [jnp.where(own_front, sib[c], own[c]) for c in range(4)]
-                merged.append([over(front[c], front[3], back[c]) for c in range(4)])
-            for c in range(4):
-                a, b = merged[0][c], merged[1][c]
-                ysend[s, 2 * m, c] = jnp.where(sub < 4, a, pltpu.roll(b, 4, 0))
-                ysend[s, 2 * m + 1, c] = jnp.where(sub < 4, pltpu.roll(a, 4, 0), b)
-        yrecv[s, y] = ysend[s, y]
-        for j in (4, 3, 5, 2, 6, 1, 7):
-            y_copy(s, j).start()
+            for i in range(0, len(level), 2):
+                lower, upper = level[i], level[i + 1]
+                w_lower = jnp.where(flip, 1.0 - upper[2], 1.0)
+                w_upper = jnp.where(flip, 1.0, 1.0 - lower[2])
+                merged.append(tuple(w_lower * a + w_upper * b for a, b in zip(lower, upper)))
+            level = merged
+        rg, ba, _ = level[0]
+        for kk in range(2):
+            piece = None
+            for c, (value, at_row) in enumerate(((rg, 0), (rg, 4), (ba, 0), (ba, 4))):
+                shift = (2 * c - at_row - 2 * kk) % 8
+                moved = pltpu.roll(value, shift, 0) if shift else value
+                piece = moved if piece is None else jnp.where(sub < 2 * c, piece, moved)
+            zsend[2 * s + kk] = piece
+            mine = jnp.logical_and(s == z, k == kk)
+
+            @pl.when(mine)
+            def _():
+                zrecv[2 * z + k] = piece
+
+            @pl.when(jnp.logical_not(mine))
+            def _():
+                pltpu.make_async_remote_copy(
+                    src_ref=zsend.at[2 * s + kk], dst_ref=zrecv.at[2 * z + k], send_sem=z_s, recv_sem=z_r,
+                    device_id=at(s, y, kk), device_id_type=MESH).start()
 
     def step(s, carry):
-        lax.fori_loop(2 * s, 2 * s + 2, shade_block, 0)
-        d_copy(s).start()
-
-        @pl.when(s >= 1)
+        @pl.when(s < STEPS)
+        def _():
+            shade_block(s)
+            d_copy(s).start()
+
+        @pl.when(s == 1)
+        def _():
+            pl.semaphore_wait(y_ready, 2)
+
+        @pl.when(jnp.logical_and(s >= 1, s < STEPS + 1))
         def _():
             merge_pack(s - 1)
-        return carry
-
-    lax.fori_loop(0, STEPS, step, 0)
-    merge_pack(STEPS - 1)
-
-    def z_target(s, ab):
-        return owner_a(z, s) if ab == 0 else owner_b(z, s)
-
-    def z_send(s, carry):
-        pltpu.make_async_copy(yrecv.at[s, pl.ds(0, 7)], yrecv.at[s, pl.ds(0, 7)], y_r.at[s]).wait()
-        level = [[yrecv[s, i, c] for c in range(4)] for i in range(8)]
-        while len(level) > 1:
-            level = [pair(level[i], level[i + 1], flip) for i in range(0, len(level), 2)]
-        total = level[0]
-        for ab in range(2):
-            for kk in range(2):
-                d = 2 * ab + kk
-                piece = pltpu.roll(total[0], (8 - 2 * d) % 8, 0) if d else total[0]
-                for c in range(1, 4):
-                    shift = (2 * c - 2 * d) % 8
-                    moved = pltpu.roll(total[c], shift, 0) if shift else total[c]
-                    piece = jnp.where(sub < 2 * c, piece, moved)
-                zsend[s, ab, kk] = piece
-                zt = z_target(s, ab)
-                mine = jnp.logical_and(zt == z, k == kk)
-
-                @pl.when(mine)
-                def _():
-                    zrecv[2 * z + k] = piece
-
-                @pl.when(jnp.logical_not(mine))
-                def _():
-                    pltpu.make_async_remote_copy(
-                        src_ref=zsend.at[s, ab, kk], dst_ref=zrecv.at[2 * z + k], send_sem=z_s, recv_sem=z_r,
-                        device_id=at(zt, y, kk), device_id_type=MESH).start()
-        return carry
-
-    lax.fori_loop(0, STEPS, z_send, 0)
+
+        @pl.when(s == LAG)
+        def _():
+            pl.semaphore_wait(z_ready, 4)
+
+        @pl.when(s >= LAG)
+        def _():
+            z_send(s - LAG)
+        return carry
+
+    lax.fori_loop(0, STEPS + LAG, step, 0)
 
     pltpu.make_async_copy(zrecv.at[pl.ds(0, 15)], zrecv.at[pl.ds(0, 15)], z_r).wait()
     for h in range(2):
@@ -333,14 +335,17 @@
 def local(density, bins, tf_color, tf_opacity, view_back):
     f32 = jnp.float32
     vmem = pl.BlockSpec(memory_space=pltpu.VMEM)
-    anyspace = pl.BlockSpec(memory_space=pl.ANY)
+    hbm = pl.BlockSpec(memory_space=pltpu.HBM)
     dma = pltpu.SemaphoreType.DMA
     result = pl.pallas_call(
         kernel,
         out_shape=jax.ShapeDtypeStruct((4, 2, 256), f32),
-        in_specs=[anyspace, anyspace, vmem, vmem, vmem],
+        in_specs=[hbm] * 5,
         out_specs=vmem,
         scratch_shapes=[
+            pltpu.VMEM((3, 256), jnp.bfloat16),
+            pltpu.VMEM((1, 256), jnp.bfloat16),
+            pltpu.VMEM((256,), jnp.int32),
             pltpu.VMEM((2, 272, 256), f32),
             pltpu.VMEM((2, 256, 256), jnp.int32),
             pltpu.VMEM((6, 256, 256), f32),
@@ -348,13 +353,13 @@
             pltpu.VMEM((2, 256, 128), f32),
             pltpu.VMEM((8, 128), f32),
             pltpu.VMEM((8, 128), f32),
-            pltpu.VMEM((STEPS, 2, 4, 2, 32, 128), f32),
-            pltpu.VMEM((STEPS, 4, 2, 32, 128), f32),
-            pltpu.VMEM((STEPS, 8, 4, 8, 128), f32),
-            pltpu.VMEM((STEPS, 8, 4, 8, 128), f32),
-            pltpu.VMEM((STEPS, 2, 2, 8, 128), f32),
+            pltpu.VMEM((STEPS, 2, 4, 32, 128), f32),
+            pltpu.VMEM((STEPS, 4, 32, 128), f32),
+            pltpu.VMEM((STEPS, 8, 2, 8, 128), f32),
+            pltpu.VMEM((STEPS, 8, 2, 8, 128), f32),
+            pltpu.VMEM((2 * STEPS, 8, 128), f32),
             pltpu.VMEM((16, 8, 128), f32),
-            dma((2,)),
+            dma((5,)),
             dma((2, 8)),
             dma((2, 8)),
             dma, dma, dma, dma,
@@ -363,9 +368,11 @@
             dma((STEPS,)),
             dma((STEPS,)),
             dma, dma,
+            pltpu.SemaphoreType.REGULAR,
+            pltpu.SemaphoreType.REGULAR,
         ],
         compiler_params=pltpu.CompilerParams(
-            collective_id=0, has_side_effects=True, vmem_limit_bytes=32 << 20),
+            collective_id=0, has_side_effects=True, vmem_limit_bytes=60 << 20),
     )(density, bins, tf_color, tf_opacity, view_back)
     return result.reshape(4, 1, 1, 2, 256)
 

time: 41.8 us -> 36.8 us (0.88)
  local copies, waits for them, and re-layouts: 4.72 us -> 1.3 us
  Pallas kernels: 36.8 us -> 35.1 us
    unnamed x11 -> x1, local copies, waits for them, and re-layouts: 4.72 us -> 1.3 us
    pallas_call x1, Pallas kernels: 36.8 us -> 35.1 us  [local(): pl.pallas_call(kernel, out_shape=jax.ShapeDtypeStruct((4, 2, 256), f32),...]
where the time goes in v2:
time: 36.8 us; the launch traced here: 36.4 us
  Pallas kernels  35.1 us (95%)
  local copies, waits for them, and re-layouts  1.3 us (4%)
    pallas_call x1, Pallas kernels, local(): pl.pallas_call(kernel, out_shape=jax.ShapeDtypeStruct((4, 2, 256), f32),...  35.1 us
    unnamed x1, local copies, waits for them, and re-layouts  1.3 us

profile of v2, /device:TPU:1, one launch (start us, length us, event | category | flops | bytes accessed | tf_op | source)
XLA Modules:
  0.0 36.4 jit_solution(1193007063105209762)
XLA Ops:
  0.0 35.1 %shard_map.55 = f32[4,2,256]{2,1,0:T(2,128)} custom-call(f32[2,256,256]{2,1,0:T(8,128)} %density.1, s32[2,256,256]{2,1,0:T(8,128)} %bins.1, bf16[3,256]{1,0:T(4,128)(2,1)} %color_h.1, bf16[1,256]{1,0:T(2,128)(2,1)} %opacity_h.1, s32[256]{0:T(256)} %view_h.1), custom_call_target="tpu_custom_call" | custom-call | tf_op jit(solution)/shard_map/pallas_call | solution.py:340
  35.1 1.3 %copy.8 = f32[4,1,1,2,256]{4,3,2,1,0:T(2,128)} copy(f32[4,1,1,2,256]{4,3,2,1,0:T(2,128)} %bitcast.3) | data formatting | bytes 16384

commit v3 on v2

--- a/solution.py
+++ b/solution.py
@@ -13,7 +13,7 @@
 
 MESH = pl.DeviceIdType.MESH
 STEPS = 8
-LAG = 4
+LAG = 8
 Y_ORDER = (0, 1, 7, 2, 6, 3, 5, 4)
 
 
@@ -24,7 +24,7 @@
 def kernel(
     density, bins, color_h, opacity_h, view_h, out,
     color, opacity, view, dens, bin_v, coef, zh, xh, xsend, xrecv, part, drecv, ysend, yrecv, zsend, zrecv,
-    in_sem, zh_s, zh_r, x_s, x_r, yh_s, yh_r, d_s, d_r, y_s, y_r, z_s, z_r, y_ready, z_ready,
+    in_sem, zh_s, zh_r, x_s, x_r, yh_s, yh_r, d_s, d_r, y_s, y_r, z_s, z_r, y_ready, z_ready, z_all,
 ):
     g = lax.axis_index("gz")
     gy = lax.axis_index("gy")
@@ -32,8 +32,10 @@
     z = lax.div(g, 16)
     y = lax.rem(lax.div(g, 2), 8)
     k = lax.rem(g, 2)
-    g_prev = lax.rem(g + 127, 128)
-    g_next = lax.rem(g + 1, 128)
+    g_prev = jnp.maximum(g - 1, 0)
+    g_next = jnp.minimum(g + 1, 127)
+    has_prev = g > 0
+    has_next = g < 127
     sibling = g + 1 - 2 * k
 
     def at(zz, yy, kk):
@@ -44,14 +46,26 @@
     def greet(target):
         pl.semaphore_signal(barrier, inc=1, device_id=target, device_id_type=MESH)
 
+    def if_z(j, do):
+        zz = jnp.clip(z + j, 0, 7)
+
+        @pl.when(zz == z + j)
+        def _():
+            do(at(zz, y, 0))
+            do(at(zz, y, 1))
+
+    def count_z(j):
+        return 2 * ((z >= j).astype(jnp.int32) + (z + j <= 7).astype(jnp.int32))
+
     greet((g, 1 - gy, gx))
-    greet((g_prev, gy, gx))
-    greet((g_next, gy, gx))
+    pl.when(has_prev)(lambda: greet((g_prev, gy, gx)))
+    pl.when(has_next)(lambda: greet((g_next, gy, gx)))
     greet((g, gy, 1 - gx))
-    for j in (1, 7, 2, 6):
+    for j in (1, 2):
         greet(at(z, lax.rem(y + j, 8), k))
-        greet(at(lax.rem(z + j, 8), y, 0))
-        greet(at(lax.rem(z + j, 8), y, 1))
+        greet(at(z, lax.rem(y + 8 - j, 8), k))
+        if_z(j, greet)
+        if_z(-j, greet)
 
     load_d = pltpu.make_async_copy(density, dens.at[:, pl.ds(8, 256), :], in_sem.at[0])
     load_b = pltpu.make_async_copy(bins, bin_v, in_sem.at[1])
@@ -63,6 +77,14 @@
     ]
     for copy in loads:
         copy.start()
+
+    @pl.when(g == 0)
+    def _():
+        zh[0] = jnp.zeros((256, 256), jnp.float32)
+
+    @pl.when(g == 127)
+    def _():
+        zh[1] = jnp.zeros((256, 256), jnp.float32)
 
     zero_row = pl.multiple_of(gy * 264, 8)
     dens[:, pl.ds(zero_row, 8), :] = jnp.zeros((2, 8, 256), jnp.float32)
@@ -119,7 +141,8 @@
 
     lax.fori_loop(0, 8, lookup_block, 0)
 
-    pl.semaphore_wait(barrier, 16)
+    pl.semaphore_wait(
+        barrier, 6 + has_prev.astype(jnp.int32) + has_next.astype(jnp.int32) + count_z(1) + count_z(2))
 
     x_copy = pltpu.make_async_remote_copy(
         src_ref=xsend, dst_ref=xrecv, send_sem=x_s, recv_sem=x_r,
@@ -143,17 +166,24 @@
             device_id=(target, gy, gx), device_id_type=MESH)
 
     def z_start(j, carry):
-        z_copy(True, j).start()
-        z_copy(False, j).start()
+        @pl.when(has_next)
+        def _():
+            z_copy(True, j).start()
+
+        @pl.when(has_prev)
+        def _():
+            z_copy(False, j).start()
         return carry
 
     lax.fori_loop(0, 8, z_start, 0)
 
+    def ready(semaphore):
+        return lambda target: pl.semaphore_signal(semaphore, inc=1, device_id=target, device_id_type=MESH)
+
     for j in (2, 6):
-        pl.semaphore_signal(y_ready, inc=1, device_id=at(z, lax.rem(y + j, 8), k), device_id_type=MESH)
-    for j in (2, 6):
-        for kk in range(2):
-            pl.semaphore_signal(z_ready, inc=1, device_id=at(lax.rem(z + j, 8), y, kk), device_id_type=MESH)
+        ready(y_ready)(at(z, lax.rem(y + j, 8), k))
+    if_z(2, ready(z_ready))
+    if_z(-2, ready(z_ready))
 
     x_copy.wait_recv()
     columns = xrecv[...]
@@ -165,11 +195,12 @@
 
     def shade_block(s):
         base = pl.multiple_of(32 * s, 32)
-        for slot in range(2):
-            pltpu.make_async_copy(
-                zh.at[slot, pl.ds(base, 32), :], zh.at[slot, pl.ds(base, 32), :], zh_r.at[slot, s]).wait()
-        first = g == 0
-        last = g == 127
+        for slot, there in ((0, has_prev), (1, has_next)):
+            @pl.when(there)
+            def _():
+                pltpu.make_async_copy(
+                    zh.at[slot, pl.ds(base, 32), :], zh.at[slot, pl.ds(base, 32), :], zh_r.at[slot, s]).wait()
+
         tiles = [[[dens[layer, pl.ds(pl.multiple_of(base + 8 * t, 8), 8), pl.ds(128 * h, 128)] for h in range(2)]
                   for t in range(6)] for layer in range(2)]
         for m in range(4):
@@ -189,9 +220,9 @@
                     below = jnp.where(sub == 7, pltpu.roll(after[h], 7, 0), pltpu.roll(here[h], 7, 0))
                     other = tiles[1 - layer][m + 1][h]
                     if layer == 0:
-                        dz = other - jnp.where(first, 0.0, zh[0, pl.ds(row, 8), cols])
+                        dz = other - zh[0, pl.ds(row, 8), cols]
                     else:
-                        dz = jnp.where(last, 0.0, zh[1, pl.ds(row, 8), cols]) - other
+                        dz = zh[1, pl.ds(row, 8), cols] - other
                     dx = right[h] - left[h]
                     dy = below - above
                     dot = dx * (0.5 * DIFFUSE * LIGHT_X) + dy * (0.5 * DIFFUSE * LIGHT_Y) + dz * (0.5 * DIFFUSE * LIGHT_Z)
@@ -283,9 +314,15 @@
         def _():
             merge_pack(s - 1)
 
+        @pl.when(s == 3)
+        def _():
+            pl.semaphore_wait(z_ready, count_z(2))
+            if_z(4, ready(z_all))
+            if_z(-4, ready(z_all))
+
         @pl.when(s == LAG)
         def _():
-            pl.semaphore_wait(z_ready, 4)
+            pl.semaphore_wait(z_all, count_z(4))
 
         @pl.when(s >= LAG)
         def _():
@@ -317,8 +354,13 @@
     yh_copy.wait_send()
 
     def z_drain(j, carry):
-        z_copy(True, j).wait_send()
-        z_copy(False, j).wait_send()
+        @pl.when(has_next)
+        def _():
+            z_copy(True, j).wait_send()
+
+        @pl.when(has_prev)
+        def _():
+            z_copy(False, j).wait_send()
         return carry
 
     lax.fori_loop(0, 8, z_drain, 0)
@@ -370,6 +412,7 @@
             dma, dma,
             pltpu.SemaphoreType.REGULAR,
             pltpu.SemaphoreType.REGULAR,
+            pltpu.SemaphoreType.REGULAR,
         ],
         compiler_params=pltpu.CompilerParams(
             collective_id=0, has_side_effects=True, vmem_limit_bytes=60 << 20),

time: 36.8 us -> 32.6 us (0.89)
  Pallas kernels: 35.1 us -> 30.9 us
    pallas_call x1, Pallas kernels: 35.1 us -> 30.9 us  [local(): pl.pallas_call(kernel, out_shape=jax.ShapeDtypeStruct((4, 2, 256), f32),...]
where the time goes in v3:
time: 32.6 us; the launch traced here: 32.2 us
  Pallas kernels  30.9 us (95%)
  local copies, waits for them, and re-layouts  1.3 us (4%)
    pallas_call x1, Pallas kernels, local(): pl.pallas_call(kernel, out_shape=jax.ShapeDtypeStruct((4, 2, 256), f32),...  30.9 us
    unnamed x1, local copies, waits for them, and re-layouts  1.3 us

profile of v3, /device:TPU:1, one launch (start us, length us, event | category | flops | bytes accessed | tf_op | source)
XLA Modules:
  0.0 32.2 jit_solution(4762491302764463408)
XLA Ops:
  0.0 30.9 %shard_map.55 = f32[4,2,256]{2,1,0:T(2,128)} custom-call(f32[2,256,256]{2,1,0:T(8,128)} %density.1, s32[2,256,256]{2,1,0:T(8,128)} %bins.1, bf16[3,256]{1,0:T(4,128)(2,1)} %color_h.1, bf16[1,256]{1,0:T(2,128)(2,1)} %opacity_h.1, s32[256]{0:T(256)} %view_h.1), custom_call_target="tpu_custom_call" | custom-call | tf_op jit(solution)/shard_map/pallas_call | solution.py:382
  30.9 1.3 %copy.8 = f32[4,1,1,2,256]{4,3,2,1,0:T(2,128)} copy(f32[4,1,1,2,256]{4,3,2,1,0:T(2,128)} %bitcast.3) | data formatting | bytes 16384

commit v4 on v3

--- a/solution.py
+++ b/solution.py
@@ -13,8 +13,8 @@
 
 MESH = pl.DeviceIdType.MESH
 STEPS = 8
-LAG = 8
-Y_ORDER = (0, 1, 7, 2, 6, 3, 5, 4)
+SIB_LAG = 2
+LAG = 7
 
 
 def over(front, front_alpha, back):
@@ -23,8 +23,8 @@
 
 def kernel(
     density, bins, color_h, opacity_h, view_h, out,
-    color, opacity, view, dens, bin_v, coef, zh, xh, xsend, xrecv, part, drecv, ysend, yrecv, zsend, zrecv,
-    in_sem, zh_s, zh_r, x_s, x_r, yh_s, yh_r, d_s, d_r, y_s, y_r, z_s, z_r, y_ready, z_ready, z_all,
+    color, opacity, view, dens, bin_v, coef, alpha, arecv, asend, yarecv, zh, xh, xsend, xrecv, part, drecv, ysend, yrecv, zsend, zrecv,
+    in_sem, zh_s, zh_r, x_s, x_r, yh_s, yh_r, d_s, d_r, y_s, y_r, z_s, z_r, a_s, a_r, ya_s, ya_r, y_ready, z_up, z_both,
 ):
     g = lax.axis_index("gz")
     gy = lax.axis_index("gy")
@@ -46,27 +46,20 @@
     def greet(target):
         pl.semaphore_signal(barrier, inc=1, device_id=target, device_id_type=MESH)
 
-    def if_z(j, do):
-        zz = jnp.clip(z + j, 0, 7)
-
-        @pl.when(zz == z + j)
-        def _():
-            do(at(zz, y, 0))
-            do(at(zz, y, 1))
-
-    def count_z(j):
-        return 2 * ((z >= j).astype(jnp.int32) + (z + j <= 7).astype(jnp.int32))
-
-    greet((g, 1 - gy, gx))
+    def each_z(do, above):
+        for j in range(1, 8):
+            zz = z + j if above else z - j
+
+            @pl.when(zz <= 7 if above else zz >= 0)
+            def _():
+                do(at(zz, y, k))
+
     pl.when(has_prev)(lambda: greet((g_prev, gy, gx)))
     pl.when(has_next)(lambda: greet((g_next, gy, gx)))
     greet((g, gy, 1 - gx))
-    for j in (1, 2):
+    for j in (2, 6, 1, 7):
         greet(at(z, lax.rem(y + j, 8), k))
-        greet(at(z, lax.rem(y + 8 - j, 8), k))
-        if_z(j, greet)
-        if_z(-j, greet)
-
+    greet((g, 1 - gy, gx))
     load_d = pltpu.make_async_copy(density, dens.at[:, pl.ds(8, 256), :], in_sem.at[0])
     load_b = pltpu.make_async_copy(bins, bin_v, in_sem.at[1])
     load_d.start()
@@ -77,6 +70,8 @@
     ]
     for copy in loads:
         copy.start()
+
+    each_z(greet, True)
 
     @pl.when(g == 0)
     def _():
@@ -136,13 +131,19 @@
                 for c in range(3):
                     coef[c, pl.ds(row, 8), cols] = k_near * near[c]
                     coef[3 + c, pl.ds(row, 8), cols] = k_far * far[c]
-                part[s, h, 3, pl.ds(8 * m, 8), :] = near[3] + (1.0 - near[3]) * far[3]
+                alpha[h, pl.ds(row, 8), :] = near[3] + (1.0 - near[3]) * far[3]
         return carry
 
     lax.fori_loop(0, 8, lookup_block, 0)
 
     pl.semaphore_wait(
-        barrier, 6 + has_prev.astype(jnp.int32) + has_next.astype(jnp.int32) + count_z(1) + count_z(2))
+        barrier, 6 + has_prev.astype(jnp.int32) + has_next.astype(jnp.int32) + z)
+
+    def ready(semaphore):
+        return lambda target: pl.semaphore_signal(semaphore, inc=1, device_id=target, device_id_type=MESH)
+
+    for j in (2, 6):
+        ready(y_ready)(at(z, lax.rem(y + j, 8), k))
 
     x_copy = pltpu.make_async_remote_copy(
         src_ref=xsend, dst_ref=xrecv, send_sem=x_s, recv_sem=x_r,
@@ -153,37 +154,67 @@
     yh_copy = pltpu.make_async_remote_copy(
         src_ref=dens.at[:, pl.ds(y_from, 8), :], dst_ref=dens.at[:, pl.ds(y_to, 8), :],
         send_sem=yh_s, recv_sem=yh_r, device_id=(g, 1 - gy, gx), device_id_type=MESH)
-    yh_copy.start()
 
     def z_copy(up, j):
         target = g_next if up else g_prev
-        row = pl.multiple_of(32 * j, 32)
+        row = pl.multiple_of(64 * j, 64)
         slot = 0 if up else 1
         return pltpu.make_async_remote_copy(
-            src_ref=dens.at[1 if up else 0, pl.ds(8 + row, 32), :],
-            dst_ref=zh.at[slot, pl.ds(row, 32), :],
+            src_ref=dens.at[1 if up else 0, pl.ds(8 + row, 64), :],
+            dst_ref=zh.at[slot, pl.ds(row, 64), :],
             send_sem=zh_s.at[slot, j], recv_sem=zh_r.at[slot, j],
             device_id=(target, gy, gx), device_id_type=MESH)
 
-    def z_start(j, carry):
+    def z_start(p, carry):
         @pl.when(has_next)
         def _():
-            z_copy(True, j).start()
+            z_copy(True, p).start()
 
         @pl.when(has_prev)
         def _():
-            z_copy(False, j).start()
+            z_copy(False, p).start()
         return carry
 
-    lax.fori_loop(0, 8, z_start, 0)
-
-    def ready(semaphore):
-        return lambda target: pl.semaphore_signal(semaphore, inc=1, device_id=target, device_id_type=MESH)
-
-    for j in (2, 6):
-        ready(y_ready)(at(z, lax.rem(y + j, 8), k))
-    if_z(2, ready(z_ready))
-    if_z(-2, ready(z_ready))
+    lax.fori_loop(0, 1, z_start, 0)
+    a_copy = pltpu.make_async_remote_copy(
+        src_ref=alpha.at[1 - k], dst_ref=arecv, send_sem=a_s, recv_sem=a_r,
+        device_id=(sibling, gy, gx), device_id_type=MESH)
+    a_copy.start()
+    yh_copy.start()
+    lax.fori_loop(1, 4, z_start, 0)
+
+    a_copy.wait_recv()
+
+    def cut(target, s, m, at_index, value):
+        target[(*at_index(2 * m),)] = value[:4]
+        target[(*at_index(2 * m + 1),)] = value[4:]
+
+    def pack_alpha(s, carry):
+        for m in range(4):
+            rows = pl.ds(pl.multiple_of(32 * s + 8 * m, 8), 8)
+            own, sib = alpha[k, rows, :], arecv[rows, :]
+            cut(asend, s, m, lambda yy: (yy, s), own + (1.0 - own) * sib)
+        return carry
+
+    lax.fori_loop(0, STEPS, pack_alpha, 0)
+    yarecv[y] = asend[y]
+
+    def ya_copy(j, late):
+        yy = lax.rem(y + j, 8)
+        blocks = pl.ds(4 * late, 4)
+        return pltpu.make_async_remote_copy(
+            src_ref=asend.at[yy, blocks], dst_ref=yarecv.at[y, blocks],
+            send_sem=ya_s.at[late], recv_sem=ya_r.at[late],
+            device_id=at(z, yy, k), device_id_type=MESH)
+
+    def ya_wait(buffer, semaphore, late):
+        arrived = buffer.at[pl.ds(0, 7), pl.ds(4 * late, 4)]
+        pltpu.make_async_copy(arrived, arrived, semaphore.at[late]).wait()
+
+    for late in range(2):
+        for j in (2, 6, 1, 7):
+            ya_copy(j, late).start()
+    each_z(ready(z_up), False)
 
     x_copy.wait_recv()
     columns = xrecv[...]
@@ -191,16 +222,17 @@
         for t in range(32):
             i = layer * 32 + t
             xh[layer, pl.ds(8 * t, 8), :] = jnp.broadcast_to(columns[:, i:i + 1], (8, 128))
-    yh_copy.wait_recv()
-
-    def shade_block(s):
-        base = pl.multiple_of(32 * s, 32)
+
+    def wait_z(s):
+        base = pl.multiple_of(64 * s, 64)
         for slot, there in ((0, has_prev), (1, has_next)):
             @pl.when(there)
             def _():
                 pltpu.make_async_copy(
-                    zh.at[slot, pl.ds(base, 32), :], zh.at[slot, pl.ds(base, 32), :], zh_r.at[slot, s]).wait()
-
+                    zh.at[slot, pl.ds(base, 64), :], zh.at[slot, pl.ds(base, 64), :], zh_r.at[slot, s]).wait()
+
+    def shade_block(s):
+        base = pl.multiple_of(32 * s, 32)
         tiles = [[[dens[layer, pl.ds(pl.multiple_of(base + 8 * t, 8), 8), pl.ds(128 * h, 128)] for h in range(2)]
                   for t in range(6)] for layer in range(2)]
         for m in range(4):
@@ -242,51 +274,81 @@
     flip = jnp.where(k == 0, flips[0].astype(jnp.int32), flips[1].astype(jnp.int32)) == 1
     own_front = jnp.where(flip, 1, 0) == k
 
-    def y_copy(s, yy):
+    def y_copy(u, first, count, yy):
+        blocks = pl.ds(first, count)
         return pltpu.make_async_remote_copy(
-            src_ref=ysend.at[s, yy], dst_ref=yrecv.at[s, y], send_sem=y_s.at[s], recv_sem=y_r.at[s],
+            src_ref=ysend.at[yy, blocks], dst_ref=yrecv.at[y, blocks], send_sem=y_s.at[u], recv_sem=y_r.at[u],
             device_id=at(z, yy, k), device_id_type=MESH)
+
+    def y_start(u, first, count):
+        for j in (4, 3, 5, 2, 6, 1, 7):
+            y_copy(u, first, count, lax.rem(y + j, 8)).start()
+
+    def y_wait(buffer, semaphore, u, first, count):
+        arrived = buffer.at[pl.ds(0, 7), pl.ds(first, count)]
+        pltpu.make_async_copy(arrived, arrived, semaphore.at[u]).wait()
 
     def merge_pack(s):
         d_copy(s).wait_recv()
         for m in range(4):
             rows = pl.ds(8 * m, 8)
-            own = [part[s, k, c, rows, :] for c in range(4)]
-            sib = [drecv[s, c, rows, :] for c in range(4)]
-            front = [jnp.where(own_front, own[c], sib[c]) for c in range(4)]
-            back = [jnp.where(own_front, sib[c], own[c]) for c in range(4)]
-            merged = [over(front[c], front[3], back[c]) for c in range(4)]
-            turned = [pltpu.roll(merged[c], 4, 0) for c in range(4)]
-            for c in range(2):
-                ysend[s, 2 * m, c] = jnp.where(sub < 4, merged[2 * c], turned[2 * c + 1])
-                ysend[s, 2 * m + 1, c] = jnp.where(sub < 4, turned[2 * c], merged[2 * c + 1])
-        yrecv[s, y] = ysend[s, y]
-        for yy in Y_ORDER:
-            @pl.when(yy != y)
-            def _():
-                y_copy(s, yy).start()
+            whole = pl.ds(pl.multiple_of(32 * s + 8 * m, 8), 8)
+            through = 1.0 - jnp.where(own_front, alpha[k, whole, :], arecv[whole, :])
+            for c in range(3):
+                own, sib = part[s, k, c, rows, :], drecv[s, c, rows, :]
+                merged = jnp.where(own_front, own, sib) + through * jnp.where(own_front, sib, own)
+                cut(ysend, s, m, lambda yy: (yy, s, c), merged)
+        yrecv[y, s] = ysend[y, s]
+
+        @pl.when(s < 2)
+        def _():
+            y_start(s, s, 1)
+
+        @pl.when(jnp.logical_and(s >= 2, lax.rem(s, 2) == 1))
+        def _():
+            y_start(lax.div(s + 3, 2) - 1, s - 1, 2)
+
+    flip4 = flip[:4]
+
+    def weigh(s):
+        alphas = [yarecv[i, s] for i in range(8)]
+        through = [1.0 - a for a in alphas]
+        before, after = [jnp.ones((4, 128), jnp.float32)], [jnp.ones((4, 128), jnp.float32)]
+        for i in range(7):
+            before.append(before[-1] * through[i])
+            after.append(after[-1] * through[7 - i])
+        while len(alphas) > 1:
+            alphas = [alphas[i] + (1.0 - alphas[i]) * alphas[i + 1] for i in range(0, len(alphas), 2)]
+        return [jnp.where(flip4, after[7 - i], before[i]) for i in range(8)], alphas[0]
 
     def z_send(s):
-        pltpu.make_async_copy(yrecv.at[s, pl.ds(0, 7)], yrecv.at[s, pl.ds(0, 7)], y_r.at[s]).wait()
-        level = []
-        for i in range(8):
-            rg, ba = yrecv[s, i, 0], yrecv[s, i, 1]
-            level.append((rg, ba, jnp.where(sub < 4, pltpu.roll(ba, 4, 0), ba)))
-        while len(level) > 1:
-            merged = []
-            for i in range(0, len(level), 2):
-                lower, upper = level[i], level[i + 1]
-                w_lower = jnp.where(flip, 1.0 - upper[2], 1.0)
-                w_upper = jnp.where(flip, 1.0, 1.0 - lower[2])
-                merged.append(tuple(w_lower * a + w_upper * b for a, b in zip(lower, upper)))
-            level = merged
-        rg, ba, _ = level[0]
+        @pl.when(s == 0)
+        def _():
+            ya_wait(yarecv, ya_r, 0)
+
+        @pl.when(s == 4)
+        def _():
+            ya_wait(yarecv, ya_r, 1)
+
+        weights, whole = weigh(s)
+
+        @pl.when(s < 2)
+        def _():
+            y_wait(yrecv, y_r, s, s, 1)
+
+        @pl.when(jnp.logical_and(s >= 2, lax.rem(s, 2) == 0))
+        def _():
+            y_wait(yrecv, y_r, lax.div(s, 2) + 1, s, 2)
+
+        total = []
+        for c in range(3):
+            terms = [weights[i] * yrecv[i, s, c] for i in range(8)]
+            while len(terms) > 1:
+                terms = [terms[i] + terms[i + 1] for i in range(0, len(terms), 2)]
+            total.append(terms[0])
+        total.append(whole)
         for kk in range(2):
-            piece = None
-            for c, (value, at_row) in enumerate(((rg, 0), (rg, 4), (ba, 0), (ba, 4))):
-                shift = (2 * c - at_row - 2 * kk) % 8
-                moved = pltpu.roll(value, shift, 0) if shift else value
-                piece = moved if piece is None else jnp.where(sub < 2 * c, piece, moved)
+            piece = jnp.concatenate([t[2 * kk:2 * kk + 2] for t in total], axis=0)
             zsend[2 * s + kk] = piece
             mine = jnp.logical_and(s == z, k == kk)
 
@@ -301,28 +363,44 @@
                     device_id=at(s, y, kk), device_id_type=MESH).start()
 
     def step(s, carry):
+        @pl.when(s == jnp.where(gy == 1, 0, STEPS - 1))
+        def _():
+            yh_copy.wait_recv()
+
+        @pl.when(jnp.logical_and(s < STEPS, lax.rem(s, 2) == 0))
+        def _():
+            wait_z(lax.div(s, 2))
+
         @pl.when(s < STEPS)
         def _():
             shade_block(s)
             d_copy(s).start()
 
-        @pl.when(s == 1)
+        @pl.when(s == 0)
         def _():
             pl.semaphore_wait(y_ready, 2)
-
-        @pl.when(jnp.logical_and(s >= 1, s < STEPS + 1))
-        def _():
-            merge_pack(s - 1)
-
-        @pl.when(s == 3)
-        def _():
-            pl.semaphore_wait(z_ready, count_z(2))
-            if_z(4, ready(z_all))
-            if_z(-4, ready(z_all))
+            for j in (4, 3, 5):
+                ya_copy(j, 0).start()
+
+        @pl.when(jnp.logical_and(s >= SIB_LAG, s < STEPS + SIB_LAG))
+        def _():
+            merge_pack(s - SIB_LAG)
+
+        @pl.when(s == SIB_LAG + 3)
+        def _():
+            for j in (4, 3, 5):
+                ya_copy(j, 1).start()
+
+        @pl.when(s == LAG - 1)
+        def _():
+            @pl.when(z < 7)
+            def _():
+                pl.semaphore_wait(z_up, 7 - z)
+            ready(z_both)((sibling, gy, gx))
 
         @pl.when(s == LAG)
         def _():
-            pl.semaphore_wait(z_all, count_z(4))
+            pl.semaphore_wait(z_both, 1)
 
         @pl.when(s >= LAG)
         def _():
@@ -363,14 +441,18 @@
             z_copy(False, j).wait_send()
         return carry
 
-    lax.fori_loop(0, 8, z_drain, 0)
+    lax.fori_loop(0, 4, z_drain, 0)
+    a_copy.wait_send()
+    for late in range(2):
+        ya_wait(asend, ya_s, late)
 
     def s_drain(s, carry):
         d_copy(s).wait_send()
-        pltpu.make_async_copy(ysend.at[s, pl.ds(0, 7)], ysend.at[s, pl.ds(0, 7)], y_s.at[s]).wait()
         return carry
 
     lax.fori_loop(0, STEPS, s_drain, 0)
+    for u, (first, count) in enumerate(((0, 1), (1, 1), (2, 2), (4, 2), (6, 2))):
+        y_wait(ysend, y_s, u, first, count)
     pltpu.make_async_copy(zrecv.at[pl.ds(0, 15)], zrecv.at[pl.ds(0, 15)], z_s).wait()
 
 
@@ -391,25 +473,31 @@
             pltpu.VMEM((2, 272, 256), f32),
             pltpu.VMEM((2, 256, 256), jnp.int32),
             pltpu.VMEM((6, 256, 256), f32),
+            pltpu.VMEM((2, 256, 128), f32),
+            pltpu.VMEM((256, 128), f32),
+            pltpu.VMEM((8, STEPS, 4, 128), f32),
+            pltpu.VMEM((8, STEPS, 4, 128), f32),
             pltpu.VMEM((2, 256, 256), f32),
             pltpu.VMEM((2, 256, 128), f32),
             pltpu.VMEM((8, 128), f32),
             pltpu.VMEM((8, 128), f32),
-            pltpu.VMEM((STEPS, 2, 4, 32, 128), f32),
-            pltpu.VMEM((STEPS, 4, 32, 128), f32),
-            pltpu.VMEM((STEPS, 8, 2, 8, 128), f32),
-            pltpu.VMEM((STEPS, 8, 2, 8, 128), f32),
+            pltpu.VMEM((STEPS, 2, 3, 32, 128), f32),
+            pltpu.VMEM((STEPS, 3, 32, 128), f32),
+            pltpu.VMEM((8, STEPS, 3, 4, 128), f32),
+            pltpu.VMEM((8, STEPS, 3, 4, 128), f32),
             pltpu.VMEM((2 * STEPS, 8, 128), f32),
             pltpu.VMEM((16, 8, 128), f32),
             dma((5,)),
-            dma((2, 8)),
-            dma((2, 8)),
+            dma((2, 4)),
+            dma((2, 4)),
             dma, dma, dma, dma,
             dma((STEPS,)),
             dma((STEPS,)),
             dma((STEPS,)),
             dma((STEPS,)),
-            dma, dma,
+            dma, dma, dma, dma,
+            dma((2,)),
+            dma((2,)),
             pltpu.SemaphoreType.REGULAR,
             pltpu.SemaphoreType.REGULAR,
             pltpu.SemaphoreType.REGULAR,

time: 32.6 us -> 31.4 us (0.963)
  the two profiles are of different devices: /device:TPU:1 before, /device:TPU:139 now
where the time goes in v4:
time: 31.4 us; the launch traced here: 31.3 us
  Pallas kernels  30 us (96%)
  local copies, waits for them, and re-layouts  1.3 us (4%)
    pallas_call x1, Pallas kernels, local(): pl.pallas_call(kernel, out_shape=jax.ShapeDtypeStruct((4, 2, 256), f32),...  30 us
    unnamed x1, local copies, waits for them, and re-layouts  1.3 us

profile of v4, /device:TPU:139, one launch (start us, length us, event | category | flops | bytes accessed | tf_op | source)
XLA Modules:
  0.0 31.3 jit_solution(4906244439191272323)
XLA Ops:
  0.0 30.0 %shard_map.55 = f32[4,2,256]{2,1,0:T(2,128)} custom-call(f32[2,256,256]{2,1,0:T(8,128)} %density.1, s32[2,256,256]{2,1,0:T(8,128)} %bins.1, bf16[3,256]{1,0:T(4,128)(2,1)} %color_h.1, bf16[1,256]{1,0:T(2,128)(2,1)} %opacity_h.1, s32[256]{0:T(256)} %view_h.1), custom_call_target="tpu_custom_call" | custom-call | tf_op jit(solution)/shard_map/pallas_call | solution.py:464
  30.0 1.3 %copy.8 = f32[4,1,1,2,256]{4,3,2,1,0:T(2,128)} copy(f32[4,1,1,2,256]{4,3,2,1,0:T(2,128)} %bitcast.3) | data formatting | bytes 16384

commit v5 on v4

--- a/solution.py
+++ b/solution.py
@@ -13,6 +13,7 @@
 
 MESH = pl.DeviceIdType.MESH
 STEPS = 8
+SENDS = ((0, 1), (1, 1), (2, 1), (3, 1), (4, 2), (6, 2))
 SIB_LAG = 2
 LAG = 7
 
@@ -134,10 +135,9 @@
                 alpha[h, pl.ds(row, 8), :] = near[3] + (1.0 - near[3]) * far[3]
         return carry
 
-    lax.fori_loop(0, 8, lookup_block, 0)
-
     pl.semaphore_wait(
         barrier, 6 + has_prev.astype(jnp.int32) + has_next.astype(jnp.int32) + z)
+
 
     def ready(semaphore):
         return lambda target: pl.semaphore_signal(semaphore, inc=1, device_id=target, device_id_type=MESH)
@@ -176,14 +176,13 @@
         return carry
 
     lax.fori_loop(0, 1, z_start, 0)
+    yh_copy.start()
+    lax.fori_loop(1, 4, z_start, 0)
+    lax.fori_loop(0, 8, lookup_block, 0)
     a_copy = pltpu.make_async_remote_copy(
         src_ref=alpha.at[1 - k], dst_ref=arecv, send_sem=a_s, recv_sem=a_r,
         device_id=(sibling, gy, gx), device_id_type=MESH)
     a_copy.start()
-    yh_copy.start()
-    lax.fori_loop(1, 4, z_start, 0)
-
-    a_copy.wait_recv()
 
     def cut(target, s, m, at_index, value):
         target[(*at_index(2 * m),)] = value[:4]
@@ -195,9 +194,6 @@
             own, sib = alpha[k, rows, :], arecv[rows, :]
             cut(asend, s, m, lambda yy: (yy, s), own + (1.0 - own) * sib)
         return carry
-
-    lax.fori_loop(0, STEPS, pack_alpha, 0)
-    yarecv[y] = asend[y]
 
     def ya_copy(j, late):
         yy = lax.rem(y + j, 8)
@@ -211,9 +207,6 @@
         arrived = buffer.at[pl.ds(0, 7), pl.ds(4 * late, 4)]
         pltpu.make_async_copy(arrived, arrived, semaphore.at[late]).wait()
 
-    for late in range(2):
-        for j in (2, 6, 1, 7):
-            ya_copy(j, late).start()
     each_z(ready(z_up), False)
 
     x_copy.wait_recv()
@@ -300,13 +293,10 @@
                 cut(ysend, s, m, lambda yy: (yy, s, c), merged)
         yrecv[y, s] = ysend[y, s]
 
-        @pl.when(s < 2)
-        def _():
-            y_start(s, s, 1)
-
-        @pl.when(jnp.logical_and(s >= 2, lax.rem(s, 2) == 1))
-        def _():
-            y_start(lax.div(s + 3, 2) - 1, s - 1, 2)
+        for u, (first, count) in enumerate(SENDS):
+            @pl.when(s == first + count - 1)
+            def _():
+                y_start(u, first, count)
 
     flip4 = flip[:4]
 
@@ -332,13 +322,10 @@
 
         weights, whole = weigh(s)
 
-        @pl.when(s < 2)
-        def _():
-            y_wait(yrecv, y_r, s, s, 1)
-
-        @pl.when(jnp.logical_and(s >= 2, lax.rem(s, 2) == 0))
-        def _():
-            y_wait(yrecv, y_r, lax.div(s, 2) + 1, s, 2)
+        for u, (first, count) in enumerate(SENDS):
+            @pl.when(s == first)
+            def _():
+                y_wait(yrecv, y_r, u, first, count)
 
         total = []
         for c in range(3):
@@ -378,9 +365,16 @@
 
         @pl.when(s == 0)
         def _():
+            a_copy.wait_recv()
+            lax.fori_loop(0, STEPS, pack_alpha, 0)
+            yarecv[y] = asend[y]
+            for j in (2, 6, 1, 7):
+                ya_copy(j, 0).start()
             pl.semaphore_wait(y_ready, 2)
             for j in (4, 3, 5):
                 ya_copy(j, 0).start()
+            for j in (2, 6, 1, 7):
+                ya_copy(j, 1).start()
 
         @pl.when(jnp.logical_and(s >= SIB_LAG, s < STEPS + SIB_LAG))
         def _():
@@ -451,7 +445,7 @@
         return carry
 
     lax.fori_loop(0, STEPS, s_drain, 0)
-    for u, (first, count) in enumerate(((0, 1), (1, 1), (2, 2), (4, 2), (6, 2))):
+    for u, (first, count) in enumerate(SENDS):
         y_wait(ysend, y_s, u, first, count)
     pltpu.make_async_copy(zrecv.at[pl.ds(0, 15)], zrecv.at[pl.ds(0, 15)], z_s).wait()
 

time: 31.4 us -> 30.3 us (0.965)
  the two profiles are of different devices: /device:TPU:139 before, /device:TPU:1 now
where the time goes in v5:
time: 30.3 us; the launch traced here: 30.1 us
  Pallas kernels  28.8 us (95%)
  local copies, waits for them, and re-layouts  1.3 us (4%)
    pallas_call x1, Pallas kernels, local(): pl.pallas_call(kernel, out_shape=jax.ShapeDtypeStruct((4, 2, 256), f32),...  28.8 us
    unnamed x1, local copies, waits for them, and re-layouts  1.3 us

profile of v5, /device:TPU:1, one launch (start us, length us, event | category | flops | bytes accessed | tf_op | source)
XLA Modules:
  0.0 30.1 jit_solution(12167299202802455853)
XLA Ops:
  0.0 28.8 %shard_map.55 = f32[4,2,256]{2,1,0:T(2,128)} custom-call(f32[2,256,256]{2,1,0:T(8,128)} %density.1, s32[2,256,256]{2,1,0:T(8,128)} %bins.1, bf16[3,256]{1,0:T(4,128)(2,1)} %color_h.1, bf16[1,256]{1,0:T(2,128)(2,1)} %opacity_h.1, s32[256]{0:T(256)} %view_h.1), custom_call_target="tpu_custom_call" | custom-call | tf_op jit(solution)/shard_map/pallas_call | solution.py:458
  28.8 1.3 %copy.8 = f32[4,1,1,2,256]{4,3,2,1,0:T(2,128)} copy(f32[4,1,1,2,256]{4,3,2,1,0:T(2,128)} %bitcast.3) | data formatting | bytes 16384

commit v6 on v5

--- a/solution.py
+++ b/solution.py
@@ -13,6 +13,7 @@
 
 MESH = pl.DeviceIdType.MESH
 STEPS = 8
+Z_GROUPS = ((0, 1), (1, 1), (2, 2), (4, 4))
 SENDS = ((0, 1), (1, 1), (2, 1), (3, 1), (4, 2), (6, 2))
 SIB_LAG = 2
 LAG = 7
@@ -42,6 +43,8 @@
     def at(zz, yy, kk):
         return ((zz * 8 + yy) * 2 + kk, gy, gx)
 
+    load_d = pltpu.make_async_copy(density, dens.at[:, pl.ds(8, 256), :], in_sem.at[0])
+    load_d.start()
     barrier = pltpu.get_barrier_semaphore()
 
     def greet(target):
@@ -55,15 +58,13 @@
             def _():
                 do(at(zz, y, k))
 
+    greet((g, 1 - gy, gx))
     pl.when(has_prev)(lambda: greet((g_prev, gy, gx)))
     pl.when(has_next)(lambda: greet((g_next, gy, gx)))
     greet((g, gy, 1 - gx))
     for j in (2, 6, 1, 7):
         greet(at(z, lax.rem(y + j, 8), k))
-    greet((g, 1 - gy, gx))
-    load_d = pltpu.make_async_copy(density, dens.at[:, pl.ds(8, 256), :], in_sem.at[0])
     load_b = pltpu.make_async_copy(bins, bin_v, in_sem.at[1])
-    load_d.start()
     load_b.start()
     loads = [
         pltpu.make_async_copy(src, dst, in_sem.at[2 + i])
@@ -142,13 +143,9 @@
     def ready(semaphore):
         return lambda target: pl.semaphore_signal(semaphore, inc=1, device_id=target, device_id_type=MESH)
 
-    for j in (2, 6):
-        ready(y_ready)(at(z, lax.rem(y + j, 8), k))
-
     x_copy = pltpu.make_async_remote_copy(
         src_ref=xsend, dst_ref=xrecv, send_sem=x_s, recv_sem=x_r,
         device_id=(g, gy, 1 - gx), device_id_type=MESH)
-    x_copy.start()
     y_from = pl.multiple_of(jnp.where(gy == 0, 256, 8), 8)
     y_to = pl.multiple_of(jnp.where(gy == 0, 0, 264), 8)
     yh_copy = pltpu.make_async_remote_copy(
@@ -157,27 +154,27 @@
 
     def z_copy(up, j):
         target = g_next if up else g_prev
-        row = pl.multiple_of(64 * j, 64)
+        first, count = Z_GROUPS[j]
+        rows = 32 * count
+        row = 32 * first
         slot = 0 if up else 1
         return pltpu.make_async_remote_copy(
-            src_ref=dens.at[1 if up else 0, pl.ds(8 + row, 64), :],
-            dst_ref=zh.at[slot, pl.ds(row, 64), :],
+            src_ref=dens.at[1 if up else 0, pl.ds(8 + row, rows), :],
+            dst_ref=zh.at[slot, pl.ds(row, rows), :],
             send_sem=zh_s.at[slot, j], recv_sem=zh_r.at[slot, j],
             device_id=(target, gy, gx), device_id_type=MESH)
 
-    def z_start(p, carry):
-        @pl.when(has_next)
-        def _():
-            z_copy(True, p).start()
-
-        @pl.when(has_prev)
-        def _():
-            z_copy(False, p).start()
-        return carry
-
-    lax.fori_loop(0, 1, z_start, 0)
+    def z_start(j):
+        pl.when(has_next)(z_copy(True, j).start)
+        pl.when(has_prev)(z_copy(False, j).start)
+
+    z_start(0)
+    x_copy.start()
+    for j in (2, 6):
+        ready(y_ready)(at(z, lax.rem(y + j, 8), k))
     yh_copy.start()
-    lax.fori_loop(1, 4, z_start, 0)
+    for j in range(1, len(Z_GROUPS)):
+        z_start(j)
     lax.fori_loop(0, 8, lookup_block, 0)
     a_copy = pltpu.make_async_remote_copy(
         src_ref=alpha.at[1 - k], dst_ref=arecv, send_sem=a_s, recv_sem=a_r,
@@ -216,13 +213,11 @@
             i = layer * 32 + t
             xh[layer, pl.ds(8 * t, 8), :] = jnp.broadcast_to(columns[:, i:i + 1], (8, 128))
 
-    def wait_z(s):
-        base = pl.multiple_of(64 * s, 64)
+    def wait_z(j):
+        first, count = Z_GROUPS[j]
         for slot, there in ((0, has_prev), (1, has_next)):
-            @pl.when(there)
-            def _():
-                pltpu.make_async_copy(
-                    zh.at[slot, pl.ds(base, 64), :], zh.at[slot, pl.ds(base, 64), :], zh_r.at[slot, s]).wait()
+            arrived = zh.at[slot, pl.ds(32 * first, 32 * count), :]
+            pl.when(there)(pltpu.make_async_copy(arrived, arrived, zh_r.at[slot, j]).wait)
 
     def shade_block(s):
         base = pl.multiple_of(32 * s, 32)
@@ -354,9 +349,10 @@
         def _():
             yh_copy.wait_recv()
 
-        @pl.when(jnp.logical_and(s < STEPS, lax.rem(s, 2) == 0))
-        def _():
-            wait_z(lax.div(s, 2))
+        for j, (first, _) in enumerate(Z_GROUPS):
+            @pl.when(s == first)
+            def _():
+                wait_z(j)
 
         @pl.when(s < STEPS)
         def _():
@@ -425,17 +421,9 @@
     x_copy.wait_send()
     yh_copy.wait_send()
 
-    def z_drain(j, carry):
-        @pl.when(has_next)
-        def _():
-            z_copy(True, j).wait_send()
-
-        @pl.when(has_prev)
-        def _():
-            z_copy(False, j).wait_send()
-        return carry
-
-    lax.fori_loop(0, 4, z_drain, 0)
+    for j in range(len(Z_GROUPS)):
+        pl.when(has_next)(z_copy(True, j).wait_send)
+        pl.when(has_prev)(z_copy(False, j).wait_send)
     a_copy.wait_send()
     for late in range(2):
         ya_wait(asend, ya_s, late)

time: 30.3 us -> 30 us (0.990)
  no operation moved by 1% of the time
where the time goes in v6:
time: 30 us; the launch traced here: 29.8 us
  Pallas kernels  28.5 us (95%)
  local copies, waits for them, and re-layouts  1.3 us (4%)
    pallas_call x1, Pallas kernels, local(): pl.pallas_call(kernel, out_shape=jax.ShapeDtypeStruct((4, 2, 256), f32),...  28.5 us
    unnamed x1, local copies, waits for them, and re-layouts  1.3 us

profile of v6, /device:TPU:1, one launch (start us, length us, event | category | flops | bytes accessed | tf_op | source)
XLA Modules:
  0.0 29.8 jit_solution(1135701127395577361)
XLA Ops:
  0.0 28.5 %shard_map.55 = f32[4,2,256]{2,1,0:T(2,128)} custom-call(f32[2,256,256]{2,1,0:T(8,128)} %density.1, s32[2,256,256]{2,1,0:T(8,128)} %bins.1, bf16[3,256]{1,0:T(4,128)(2,1)} %color_h.1, bf16[1,256]{1,0:T(2,128)(2,1)} %opacity_h.1, s32[256]{0:T(256)} %view_h.1), custom_call_target="tpu_custom_call" | custom-call | tf_op jit(solution)/shard_map/pallas_call | solution.py:446
  28.5 1.3 %copy.8 = f32[4,1,1,2,256]{4,3,2,1,0:T(2,128)} copy(f32[4,1,1,2,256]{4,3,2,1,0:T(2,128)} %bitcast.3) | data formatting | bytes 16384

commit v7 on v6

--- a/solution.py
+++ b/solution.py
@@ -168,8 +168,11 @@
         pl.when(has_next)(z_copy(True, j).start)
         pl.when(has_prev)(z_copy(False, j).start)
 
-    z_start(0)
+    pl.when(jnp.logical_and(has_next, k == 1))(z_copy(True, 0).start)
+    pl.when(jnp.logical_and(has_prev, k == 0))(z_copy(False, 0).start)
     x_copy.start()
+    pl.when(k == 0)(z_copy(True, 0).start)
+    pl.when(k == 1)(z_copy(False, 0).start)
     for j in (2, 6):
         ready(y_ready)(at(z, lax.rem(y + j, 8), k))
     yh_copy.start()
@@ -204,7 +207,6 @@
         arrived = buffer.at[pl.ds(0, 7), pl.ds(4 * late, 4)]
         pltpu.make_async_copy(arrived, arrived, semaphore.at[late]).wait()
 
-    each_z(ready(z_up), False)
 
     x_copy.wait_recv()
     columns = xrecv[...]
@@ -361,6 +363,7 @@
 
         @pl.when(s == 0)
         def _():
+            each_z(ready(z_up), False)
             a_copy.wait_recv()
             lax.fori_loop(0, STEPS, pack_alpha, 0)
             yarecv[y] = asend[y]

time: 30 us -> 30.1 us (level)
  no operation moved by 1% of the time
where the time goes in v7:
time: 30.1 us; the launch traced here: 29.9 us
  Pallas kernels  28.6 us (95%)
  local copies, waits for them, and re-layouts  1.3 us (4%)
    pallas_call x1, Pallas kernels, local(): pl.pallas_call(kernel, out_shape=jax.ShapeDtypeStruct((4, 2, 256), f32),...  28.6 us
    unnamed x1, local copies, waits for them, and re-layouts  1.3 us

profile of v7, /device:TPU:1, one launch (start us, length us, event | category | flops | bytes accessed | tf_op | source)
XLA Modules:
  0.0 29.9 jit_solution(9463287170600646519)
XLA Ops:
  0.0 28.6 %shard_map.55 = f32[4,2,256]{2,1,0:T(2,128)} custom-call(f32[2,256,256]{2,1,0:T(8,128)} %density.1, s32[2,256,256]{2,1,0:T(8,128)} %bins.1, bf16[3,256]{1,0:T(4,128)(2,1)} %color_h.1, bf16[1,256]{1,0:T(2,128)(2,1)} %opacity_h.1, s32[256]{0:T(256)} %view_h.1), custom_call_target="tpu_custom_call" | custom-call | tf_op jit(solution)/shard_map/pallas_call | solution.py:449
  28.6 1.3 %copy.8 = f32[4,1,1,2,256]{4,3,2,1,0:T(2,128)} copy(f32[4,1,1,2,256]{4,3,2,1,0:T(2,128)} %bitcast.3) | data formatting | bytes 16384

commit v8 on v6

--- a/solution.py
+++ b/solution.py
@@ -15,8 +15,8 @@
 STEPS = 8
 Z_GROUPS = ((0, 1), (1, 1), (2, 2), (4, 4))
 SENDS = ((0, 1), (1, 1), (2, 1), (3, 1), (4, 2), (6, 2))
-SIB_LAG = 2
-LAG = 7
+SIB_LAG = 1
+LAG = 8
 
 
 def over(front, front_alpha, back):
@@ -362,19 +362,24 @@
         @pl.when(s == 0)
         def _():
             a_copy.wait_recv()
-            lax.fori_loop(0, STEPS, pack_alpha, 0)
-            yarecv[y] = asend[y]
+            lax.fori_loop(0, 4, pack_alpha, 0)
+            yarecv[y, pl.ds(0, 4)] = asend[y, pl.ds(0, 4)]
             for j in (2, 6, 1, 7):
                 ya_copy(j, 0).start()
             pl.semaphore_wait(y_ready, 2)
             for j in (4, 3, 5):
                 ya_copy(j, 0).start()
+
+        @pl.when(jnp.logical_and(s >= SIB_LAG, s < STEPS + SIB_LAG))
+        def _():
+            merge_pack(s - SIB_LAG)
+
+        @pl.when(s == SIB_LAG)
+        def _():
+            lax.fori_loop(4, STEPS, pack_alpha, 0)
+            yarecv[y, pl.ds(4, 4)] = asend[y, pl.ds(4, 4)]
             for j in (2, 6, 1, 7):
                 ya_copy(j, 1).start()
-
-        @pl.when(jnp.logical_and(s >= SIB_LAG, s < STEPS + SIB_LAG))
-        def _():
-            merge_pack(s - SIB_LAG)
 
         @pl.when(s == SIB_LAG + 3)
         def _():

time: 30 us -> 29.7 us (0.990)
  Pallas kernels: 28.5 us -> 28.2 us
    pallas_call x1, Pallas kernels: 28.5 us -> 28.2 us  [local(): pl.pallas_call(kernel, out_shape=jax.ShapeDtypeStruct((4, 2, 256), f32),...]
where the time goes in v8:
time: 29.7 us; the launch traced here: 29.5 us
  Pallas kernels  28.2 us (95%)
  local copies, waits for them, and re-layouts  1.3 us (4%)
    pallas_call x1, Pallas kernels, local(): pl.pallas_call(kernel, out_shape=jax.ShapeDtypeStruct((4, 2, 256), f32),...  28.2 us
    unnamed x1, local copies, waits for them, and re-layouts  1.3 us

profile of v8, /device:TPU:1, one launch (start us, length us, event | category | flops | bytes accessed | tf_op | source)
XLA Modules:
  0.0 29.5 jit_solution(18185417869041607107)
XLA Ops:
  0.0 28.2 %shard_map.55 = f32[4,2,256]{2,1,0:T(2,128)} custom-call(f32[2,256,256]{2,1,0:T(8,128)} %density.1, s32[2,256,256]{2,1,0:T(8,128)} %bins.1, bf16[3,256]{1,0:T(4,128)(2,1)} %color_h.1, bf16[1,256]{1,0:T(2,128)(2,1)} %opacity_h.1, s32[256]{0:T(256)} %view_h.1), custom_call_target="tpu_custom_call" | custom-call | tf_op jit(solution)/shard_map/pallas_call | solution.py:451
  28.2 1.3 %copy.8 = f32[4,1,1,2,256]{4,3,2,1,0:T(2,128)} copy(f32[4,1,1,2,256]{4,3,2,1,0:T(2,128)} %bitcast.3) | data formatting | bytes 16384
